TPU v7x, 32 devices: a whole 2x2x4 slice. The times are simulated.
32 devices in a mesh: view: 4 (over y, x), xy: 4 (over z), gz: 2 (over core).
Axes of the slice: x: 2, y: 2, z: 4, core: 2. Of those that a mesh axis runs over, the one named last changes fastest.
Arguments:
- estimate: float32 [64, 256, 128], P('gz', 'xy'), may hold values from 0.5 to 2
- views: bfloat16 [4, 64, 256, 128], P('view', 'gz', 'xy'), may hold values from 0.19921875 to 3
- shifts: int32 [4, 3], P('view'), may hold values from -32 to 32, as said below
- kernels: float32 [4, 3, 63], P('view'), may hold values from 0.02 to 1
- coverage: int32 [4, 2, 1], replicated, may hold values from 0 to 1, as said below
Outputs:
- refined: float32 [64, 256, 128], P('gz', 'xy')
Inputs may be any that keep to these rules, and one draw needn't show every extreme that they name: `shifts`: both ends -32 and 32 occur in every draw. `coverage`: every block is covered by at least one view.
All inputs are finite; a program needn't handle non-finite values.
Results may differ from a plain program's by a relative error of at most 0.0003.
Values may be sent and summed in bfloat16 or wider, within the bound.
A program may use at most 64 MiB of HBM per device.

v0:
```python
import jax
import jax.numpy as jnp
from jax import lax
from jax.sharding import PartitionSpec as P

SHIFT = 32
BLOCK = 128
ITERS = 2


def extended(cells, sides, width):
    for axis, dim in sides:
        count = lax.axis_size(axis)
        ends = count - 1
        head = lax.slice_in_dim(cells, 0, width, axis=dim)
        tail = lax.slice_in_dim(cells, cells.shape[dim] - width, cells.shape[dim], axis=dim)
        cells = jnp.concatenate(
            [
                lax.ppermute(tail, axis, [(i, (i + 1) % count) for i in range(ends)]),
                cells,
                lax.ppermute(head, axis, [((i + 1) % count, i) for i in range(ends)]),
            ],
            axis=dim,
        )
    return cells


def band(kern, rows, cols, offset):
    row_ids = lax.broadcasted_iota(jnp.int32, (rows, cols), 0)
    col_ids = lax.broadcasted_iota(jnp.int32, (rows, cols), 1)
    offsets = row_ids - col_ids + offset

    def add_tap(tap_index, summed):
        return summed + jnp.where(offsets == tap_index, kern[tap_index], 0.0)

    return lax.fori_loop(0, kern.shape[0], add_tap, jnp.zeros((rows, cols), jnp.float32))


def along_x(vol, matrix):
    return jnp.einsum("zyx,xk->zyk", vol, matrix, precision=lax.Precision.HIGHEST)


def along_rows(vol, rim_mat, half):
    padded = extended(vol.astype(jnp.bfloat16), (("xy", 1),), half).astype(vol.dtype)
    return jnp.einsum("zyx,yk->zkx", padded, rim_mat, precision=lax.Precision.HIGHEST)


def along_planes(vol, matrix, half):
    padded = extended(vol, (("gz", 0),), half)
    return jnp.einsum("zyx,zk->kyx", padded, matrix, precision=lax.Precision.HIGHEST)


def on_device(estimate, views, shifts, kernels, coverage):
    slab, strip, width = estimate.shape
    taps = kernels.shape[2]
    half = (taps - 1) // 2
    psf = kernels[0] / jnp.sum(kernels[0], axis=1, keepdims=True)
    raw = views[0]
    margin = SHIFT
    padded = extended(raw, (("gz", 0), ("xy", 1)), margin)
    padded = jnp.pad(padded, ((0, 0), (0, 0), (margin, margin)))
    start = margin + shifts[0]
    data = lax.dynamic_slice(padded, (start[0], start[1], start[2]), (slab, strip, width)).astype(
        jnp.float32
    )
    field = estimate
    row_first = lax.axis_index("xy") * strip
    planes = field.shape[0]
    mats = []
    for reverse in (False, True):
        rows_psf = psf[:, ::-1] if reverse else psf
        x_mat = band(rows_psf[2], width, width, half)
        z_mat = band(rows_psf[0], planes + 2 * half, planes, 0)
        rim_mat = band(rows_psf[1], strip + 2 * half, strip, 0)
        mats.append((x_mat, None, rim_mat, z_mat))
    row_global = row_first + lax.broadcasted_iota(jnp.int32, (strip,), 0)
    row_onehot = (row_global[:, None] // BLOCK == jnp.arange(coverage.shape[1])[None]).astype(
        jnp.float32
    )
    col_onehot = (
        jnp.arange(width)[:, None] // BLOCK == jnp.arange(coverage.shape[2])[None]
    ).astype(jnp.float32)
    grid = jnp.einsum("vbc,yb,xc->vyx", coverage.astype(jnp.float32), row_onehot, col_onehot)
    mine = lax.dynamic_index_in_dim(grid, lax.axis_index("view"), 0, keepdims=False)
    count = jnp.sum(grid, axis=0)
    for step in range(ITERS):
        predicted = along_x(field, mats[0][0])
        predicted = along_rows(predicted, mats[0][2], half)
        predicted = along_planes(predicted, mats[0][3], half)
        ratio = data / (predicted + 0.05)
        back = along_x(ratio, mats[1][0])
        back = along_rows(back, mats[1][2], half)
        back = along_planes(back, mats[1][3], half)
        term = mine[None] * back
        total = lax.psum(term, "view")
        field = field * total / count[None]
    return field


def solution(mesh):
    placed = (
        P("gz", "xy", None),
        P("view", "gz", "xy", None),
        P("view", None),
        P("view", None, None),
        P(),
    )
    return jax.shard_map(
        on_device, mesh=mesh, in_specs=placed, out_specs=P("gz", "xy", None), check_vma=False
    )
```

profile of v0, /device:TPU:9, one launch (start us, length us, event | category | flops | bytes accessed | tf_op | source)
XLA Modules:
  0.0 734.8 jit_solution(2234918622438220461)
XLA Ops:
  12.0 79.5 %while.88 = (s32[]{:T(128)}, f32[128,128]{1,0:T(8,128)S(1)}, f32[63]{0:T(128)S(1)}, s32[]{:T(128)}, s32[]{:T(128)}) while((s32[]{:T(128)}, f32[128,128]{1,0:T(8,128)S(1)}, f32[63]{0:T(128)S(1)}, s32[]{:T(128)}, s32[]{:T(128)}) %tuple.185), condition=%wide.region_10.11_spmd.clone, body=%wide.region_9.10_spmd.clone.sunk | while | flops 98307 | bytes 131171 | solution.py:36
  95.8 3.4 collective-permute-start.4
  99.1 81.4 %while.87 = (s32[]{:T(128)}, f32[126,64]{1,0:T(8,128)S(1)}, f32[63]{0:T(128)S(1)}, s32[]{:T(128)}, s32[]{:T(128)}) while((s32[]{:T(128)}, f32[126,64]{1,0:T(8,128)S(1)}, f32[63]{0:T(128)S(1)}, s32[]{:T(128)}, s32[]{:T(128)}) %tuple.188), condition=%wide.region_8.9_spmd.clone, body=%wide.region_7.8_spmd.clone.sunk | while | flops 40323 | bytes 64611 | solution.py:36
  180.7 80.4 %while.89 = (s32[]{:T(128)}, f32[128,128]{1,0:T(8,128)S(1)}, f32[63]{0:T(128)S(1)}, s32[]{:T(128)}, s32[]{:T(128)}) while((s32[]{:T(128)}, f32[128,128]{1,0:T(8,128)S(1)}, f32[63]{0:T(128)S(1)}, s32[]{:T(128)}, s32[]{:T(128)}) %tuple.209), condition=%wide.region_12.13_spmd.clone, body=%wide.region_11.12_spmd.clone.sunk | while | flops 98307 | bytes 131171 | solution.py:36
  261.1 79.9 %while.86 = (s32[]{:T(128)}, f32[94,32]{1,0:T(8,128)S(1)}, f32[63]{0:T(128)S(1)}, s32[]{:T(128)}, s32[]{:T(128)}) while((s32[]{:T(128)}, f32[94,32]{1,0:T(8,128)S(1)}, f32[63]{0:T(128)S(1)}, s32[]{:T(128)}, s32[]{:T(128)}) %tuple.191), condition=%wide.region_6.7_spmd.clone, body=%wide.region_5.6_spmd.clone.sunk | while | flops 15043 | bytes 24163 | solution.py:36
  343.3 4.7 collective-permute-start.7
  349.4 4.2 iota_compare_fusion
  357.2 3.5 collective-permute-start.2
  369.2 3.4 fusion.14
  376.3 6.5 fusion.60
  386.5 3.6 collective-permute-start.8
  390.1 80.4 %while.85 = (s32[]{:T(128)}, f32[126,64]{1,0:T(8,128)S(1)}, f32[63]{0:T(128)S(1)}, s32[]{:T(128)}, s32[]{:T(128)}) while((s32[]{:T(128)}, f32[126,64]{1,0:T(8,128)S(1)}, f32[63]{0:T(128)S(1)}, s32[]{:T(128)}, s32[]{:T(128)}) %tuple.207), condition=%wide.region_4.5_spmd.clone, body=%wide.region_3.4_spmd.clone.sunk | while | flops 40323 | bytes 64611 | solution.py:36
  472.9 5.6 collective-permute-start.11
  479.8 79.2 %while.84 = (s32[]{:T(128)}, f32[94,32]{1,0:T(8,128)S(1)}, f32[63]{0:T(128)S(1)}, s32[]{:T(128)}, s32[]{:T(128)}) while((s32[]{:T(128)}, f32[94,32]{1,0:T(8,128)S(1)}, f32[63]{0:T(128)S(1)}, s32[]{:T(128)}, s32[]{:T(128)}) %tuple.208), condition=%wide.region_2.3_spmd.clone, body=%wide.region_1.2_spmd.clone.sunk | while | flops 15043 | bytes 24163 | solution.py:36
  559.8 4.3 fusion.20
  564.2 53.5 %all-reduce.4.cloned.1.call-done = f32[32,64,128]{2,0,1:T(8,128)} async-done(((f32[32,64,128]{2,0,1:T(8,128)}), f32[32,64,128]{2,0,1:T(8,128)}) %all-reduce.4.cloned.1.call-update) | async-done | bytes 1048592 | tf_op jit(solution)/shard_map/psum | solution.py:95
  623.6 3.1 collective-permute-start.12
  626.7 3.8 collective-permute-done.13
  633.3 3.8 collective-permute-start.15
  642.1 3.4 fusion.12
  649.2 3.4 collective-permute-start.16
  652.6 4.4 collective-permute-done.17
  667.7 4.3 fusion.23
  672.0 52.5 %all-reduce.6.cloned.1.call-done = f32[32,64,128]{2,0,1:T(8,128)} async-done(((f32[32,64,128]{2,0,1:T(8,128)}), f32[32,64,128]{2,0,1:T(8,128)}) %all-reduce.6.cloned.1.call-update) | async-done | bytes 1048592 | tf_op jit(solution)/shard_map/psum | solution.py:95
  (847 shorter events, 534.8 us)
Async XLA Ops:
  6.5 611.2 %all-reduce.4.cloned.1.call-start = ((), (), s32[]{:S(2)}) async-start(), calls=%async_computation | async-start | bytes 2097152 | tf_op jit(solution)/shard_map/psum | solution.py:95
  6.5 347.0 %collective-permute-start.1 = (bf16[32,64,128]{2,1,0:T(8,128)(2,1)}, bf16[32,64,128]{2,1,0:T(8,128)(2,1)S(1)}, u32[]{:S(2)}, u32[]{:S(2)}) collective-permute-start(bf16[32,64,128]{2,1,0:T(8,128)(2,1)} %bitcast.81), channel_id=1, source_target_pairs={{1,0},{3,2},{5,4},{7,6},{9,8},{11,10},{13,12},{15,14},{17,16},{19,... | collective-permute-start | bytes 1572872 | tf_op jit(solution)/shard_map/ppermute | solution.py:21
  9.1 344.4 %collective-permute-start = (bf16[32,64,128]{2,1,0:T(8,128)(2,1)}, bf16[32,64,128]{2,1,0:T(8,128)(2,1)S(1)}, u32[]{:S(2)}, u32[]{:S(2)}) collective-permute-start(bf16[32,64,128]{2,1,0:T(8,128)(2,1)} %bitcast.82), channel_id=1, source_target_pairs={{0,1},{2,3},{4,5},{6,7},{8,9},{10,11},{12,13},{14,15},{16,17},{18,... | collective-permute-start | bytes 1572872 | tf_op jit(solution)/shard_map/ppermute | solution.py:19
  93.8 247.2 %collective-permute-start.5 = (bf16[32,31,128]{2,1,0:T(8,128)(2,1)S(1)}, bf16[32,31,128]{2,1,0:T(8,128)(2,1)S(1)}, u32[]{:S(2)}, u32[]{:S(2)}) collective-permute-start(bf16[32,31,128]{2,1,0:T(8,128)(2,1)S(1)} %get-tuple-element.622), channel_id=1, source_target_pairs={{2,0},{4,2},{6,4},{3,1},{5,3},{7,5},{10,8},{12,10},{14,12},{11,9},... | collective-permute-start | bytes 761864 | tf_op jit(solution)/shard_map/ppermute | solution.py:21
  95.8 245.3 %collective-permute-start.4 = (bf16[32,31,128]{2,1,0:T(8,128)(2,1)S(1)}, bf16[32,31,128]{2,1,0:T(8,128)(2,1)S(1)}, u32[]{:S(2)}, u32[]{:S(2)}) collective-permute-start(bf16[32,31,128]{2,1,0:T(8,128)(2,1)S(1)} %get-tuple-element.621), channel_id=1, source_target_pairs={{0,2},{2,4},{4,6},{1,3},{3,5},{5,7},{8,10},{10,12},{12,14},{9,11},... | collective-permute-start | bytes 761864 | tf_op jit(solution)/shard_map/ppermute | solution.py:19
  343.3 24.0 %collective-permute-start.7 = (f32[31,64,128]{2,1,0:T(8,128)}, f32[31,64,128]{2,1,0:T(8,128)}, u32[]{:S(2)}, u32[]{:S(2)}) collective-permute-start(f32[31,64,128]{2,1,0:T(8,128)} %get-tuple-element.614), channel_id=1, source_target_pairs={{1,0},{3,2},{5,4},{7,6},{9,8},{11,10},{13,12},{15,14},{17,16},{19,... | collective-permute-start | bytes 3047432 | tf_op jit(solution)/shard_map/ppermute | solution.py:21
  348.0 19.3 %collective-permute-start.6 = (f32[31,64,128]{2,1,0:T(8,128)}, f32[31,64,128]{2,1,0:T(8,128)}, u32[]{:S(2)}, u32[]{:S(2)}) collective-permute-start(f32[31,64,128]{2,1,0:T(8,128)} %get-tuple-element.613), channel_id=1, source_target_pairs={{0,1},{2,3},{4,5},{6,7},{8,9},{10,11},{12,13},{14,15},{16,17},{18,... | collective-permute-start | bytes 3047432 | tf_op jit(solution)/shard_map/ppermute | solution.py:19
  355.2 19.1 %collective-permute-start.3 = (bf16[96,32,128]{2,1,0:T(8,128)(2,1)}, bf16[96,32,128]{2,1,0:T(8,128)(2,1)}, u32[]{:S(2)}, u32[]{:S(2)}) collective-permute-start(bf16[96,32,128]{2,1,0:T(8,128)(2,1)} %get-tuple-element.606), channel_id=1, source_target_pairs={{2,0},{4,2},{6,4},{3,1},{5,3},{7,5},{10,8},{12,10},{14,12},{11,9},... | collective-permute-start | bytes 2359304 | tf_op jit(solution)/shard_map/ppermute | solution.py:21
  357.2 19.1 %collective-permute-start.2 = (bf16[96,32,128]{2,1,0:T(8,128)(2,1)}, bf16[96,32,128]{2,1,0:T(8,128)(2,1)}, u32[]{:S(2)}, u32[]{:S(2)}) collective-permute-start(bf16[96,32,128]{2,1,0:T(8,128)(2,1)} %get-tuple-element.605), channel_id=1, source_target_pairs={{0,2},{2,4},{4,6},{1,3},{3,5},{5,7},{8,10},{10,12},{12,14},{9,11},... | collective-permute-start | bytes 2359304 | tf_op jit(solution)/shard_map/ppermute | solution.py:19
  384.5 86.1 %collective-permute-start.9 = (bf16[32,31,128]{2,1,0:T(8,128)(2,1)S(1)}, bf16[32,31,128]{2,1,0:T(8,128)(2,1)S(1)}, u32[]{:S(2)}, u32[]{:S(2)}) collective-permute-start(bf16[32,31,128]{2,1,0:T(8,128)(2,1)S(1)} %get-tuple-element.620), channel_id=1, source_target_pairs={{2,0},{4,2},{6,4},{3,1},{5,3},{7,5},{10,8},{12,10},{14,12},{11,9},... | collective-permute-start | bytes 761864 | tf_op jit(solution)/shard_map/ppermute | solution.py:21
  386.5 84.1 %collective-permute-start.8 = (bf16[32,31,128]{2,1,0:T(8,128)(2,1)S(1)}, bf16[32,31,128]{2,1,0:T(8,128)(2,1)S(1)}, u32[]{:S(2)}, u32[]{:S(2)}) collective-permute-start(bf16[32,31,128]{2,1,0:T(8,128)(2,1)S(1)} %get-tuple-element.619), channel_id=1, source_target_pairs={{0,2},{2,4},{4,6},{1,3},{3,5},{5,7},{8,10},{10,12},{12,14},{9,11},... | collective-permute-start | bytes 761864 | tf_op jit(solution)/shard_map/ppermute | solution.py:19
  470.6 88.4 %copy-start.4 = (s32[4,2,1]{0,2,1:T(1,128)S(1)}, s32[4,2,1]{0,2,1:T(1,128)}, u32[]{:S(2)}) copy-start(s32[4,2,1]{0,2,1:T(1,128)} %param.21) | copy-start | bytes 100
  472.9 86.5 %collective-permute-start.11 = (f32[31,64,128]{2,1,0:T(8,128)}, f32[31,64,128]{2,1,0:T(8,128)S(1)}, u32[]{:S(2)}, u32[]{:S(2)}) collective-permute-start(f32[31,64,128]{2,1,0:T(8,128)} %get-tuple-element.612), channel_id=1, source_target_pairs={{1,0},{3,2},{5,4},{7,6},{9,8},{11,10},{13,12},{15,14},{17,16},{19,... | collective-permute-start | bytes 3047432 | tf_op jit(solution)/shard_map/ppermute | solution.py:21
  478.5 80.9 %collective-permute-start.10 = (f32[31,64,128]{2,1,0:T(8,128)}, f32[31,64,128]{2,1,0:T(8,128)S(1)}, u32[]{:S(2)}, u32[]{:S(2)}) collective-permute-start(f32[31,64,128]{2,1,0:T(8,128)} %get-tuple-element.611), channel_id=1, source_target_pairs={{0,1},{2,3},{4,5},{6,7},{8,9},{10,11},{12,13},{14,15},{16,17},{18,... | collective-permute-start | bytes 3047432 | tf_op jit(solution)/shard_map/ppermute | solution.py:19
  559.8 57.9 %copy-start = (f32[32,64,128]{2,1,0:T(8,128)S(1)}, f32[32,64,128]{2,1,0:T(8,128)}, u32[]{:S(2)}) copy-start(f32[32,64,128]{2,1,0:T(8,128)} %param.17) | copy-start | bytes 3145732
  564.2 160.3 %all-reduce.6.cloned.1.call-start = ((), (), s32[]{:S(2)}) async-start(), calls=%async_computation.1 | async-start | bytes 2097152 | tf_op jit(solution)/shard_map/psum | solution.py:95
  621.4 9.1 %collective-permute-start.13 = (bf16[32,31,128]{2,1,0:T(8,128)(2,1)S(1)}, bf16[32,31,128]{2,1,0:T(8,128)(2,1)S(1)}, u32[]{:S(2)}, u32[]{:S(2)}) collective-permute-start(bf16[32,31,128]{2,1,0:T(8,128)(2,1)S(1)} %get-tuple-element.618), channel_id=1, source_target_pairs={{2,0},{4,2},{6,4},{3,1},{5,3},{7,5},{10,8},{12,10},{14,12},{11,9},... | collective-permute-start | bytes 761864 | tf_op jit(solution)/shard_map/ppermute | solution.py:21
  623.6 8.8 %collective-permute-start.12 = (bf16[32,31,128]{2,1,0:T(8,128)(2,1)S(1)}, bf16[32,31,128]{2,1,0:T(8,128)(2,1)S(1)}, u32[]{:S(2)}, u32[]{:S(2)}) collective-permute-start(bf16[32,31,128]{2,1,0:T(8,128)(2,1)S(1)} %get-tuple-element.617), channel_id=1, source_target_pairs={{0,2},{2,4},{4,6},{1,3},{3,5},{5,7},{8,10},{10,12},{12,14},{9,11},... | collective-permute-start | bytes 761864 | tf_op jit(solution)/shard_map/ppermute | solution.py:19
  633.3 6.0 collective-permute-start.15
  637.1 4.5 collective-permute-start.14
  647.3 9.7 %collective-permute-start.17 = (bf16[32,31,128]{2,1,0:T(8,128)(2,1)S(1)}, bf16[32,31,128]{2,1,0:T(8,128)(2,1)S(1)}, u32[]{:S(2)}, u32[]{:S(2)}) collective-permute-start(bf16[32,31,128]{2,1,0:T(8,128)(2,1)S(1)} %get-tuple-element.616), channel_id=1, source_target_pairs={{2,0},{4,2},{6,4},{3,1},{5,3},{7,5},{10,8},{12,10},{14,12},{11,9},... | collective-permute-start | bytes 761864 | tf_op jit(solution)/shard_map/ppermute | solution.py:21
  649.2 9.7 %collective-permute-start.16 = (bf16[32,31,128]{2,1,0:T(8,128)(2,1)S(1)}, bf16[32,31,128]{2,1,0:T(8,128)(2,1)S(1)}, u32[]{:S(2)}, u32[]{:S(2)}) collective-permute-start(bf16[32,31,128]{2,1,0:T(8,128)(2,1)S(1)} %get-tuple-element.615), channel_id=1, source_target_pairs={{0,2},{2,4},{4,6},{1,3},{3,5},{5,7},{8,10},{10,12},{12,14},{9,11},... | collective-permute-start | bytes 761864 | tf_op jit(solution)/shard_map/ppermute | solution.py:19
  659.8 5.1 collective-permute-start.19
  662.8 4.5 collective-permute-start.18
  (4 other events, 17.9 us)
Sparse Core Ops, SparseCore 0:
  564.3 53.3 all-reduce.3
  672.1 52.2 all-reduce.5
where the time goes:
time: 748 us; the launch traced here: 735 us
  other arithmetic  266 us (36%)
  local copies, waits for them, and re-layouts  233 us (31%)
  waiting for transfers between devices  128 us (17%)
  starting transfers between devices  53.3 us (7%)
  matrix products  25.7 us (3%)
  between operations  20.2 us (3%)
  loops' own time  8.59 us (1%)
    add x378, other arithmetic, add_tap(): return summed + jnp.where(offsets == tap_index, kern[tap_index], 0.0)  247 us
    dynamic_slice x378, local copies, waits for them, and re-layouts, add_tap(): return summed + jnp.where(offsets == tap_index, kern[tap_index], 0.0)  225 us
    psum x2, waiting for transfers between devices, on_device(): total = lax.psum(term, 'view')  106 us
    ppermute x10, starting transfers between devices, extended(): lax.ppermute(head, axis, [((i + 1) % count, i) for i in range(ends)])  29.5 us
    ppermute x10, starting transfers between devices, extended(): lax.ppermute(tail, axis, [(i, (i + 1) % count) for i in range(ends)])  23.8 us
    dot_general x4, matrix products, along_planes(): jnp.einsum('zyx,zk->kyx', padded, matrix, precision=lax.Precision.HIGHEST)  15.4 us
  transfers between devices with their start and end apart: 22, of which 12 were waited for; matrix products, arithmetic and copies ran while one was open for 67% of the time, Pallas kernels for 0%

commit v1 on v0

--- a/solution.py
+++ b/solution.py
@@ -30,10 +30,9 @@
     col_ids = lax.broadcasted_iota(jnp.int32, (rows, cols), 1)
     offsets = row_ids - col_ids + offset
 
-    def add_tap(tap_index, summed):
-        return summed + jnp.where(offsets == tap_index, kern[tap_index], 0.0)
-
-    return lax.fori_loop(0, kern.shape[0], add_tap, jnp.zeros((rows, cols), jnp.float32))
+    taps = kern.shape[0]
+    tap_ids = lax.broadcasted_iota(jnp.int32, (taps, rows, cols), 0)
+    return jnp.sum(jnp.where(offsets[None] == tap_ids, kern[:, None, None], 0.0), axis=0)
 
 
 def along_x(vol, matrix):

time: 748 us -> 276 us (0.37)
  the two profiles are of different devices: /device:TPU:9 before, /device:TPU:0 now
where the time goes in v1:
time: 276 us; the launch traced here: 271 us
  waiting for transfers between devices  140 us (51%)
  starting transfers between devices  56.9 us (21%)
  matrix products  26.8 us (10%)
  other arithmetic  20.4 us (7%)
  between operations  20.1 us (7%)
  local copies, waits for them, and re-layouts  6.82 us (2%)
    psum x2, waiting for transfers between devices, on_device(): total = lax.psum(term, 'view')  110 us
    ppermute x10, starting transfers between devices, extended(): lax.ppermute(tail, axis, [(i, (i + 1) % count) for i in range(ends)])  43.9 us
    ppermute x10, waiting for transfers between devices, extended(): lax.ppermute(head, axis, [((i + 1) % count, i) for i in range(ends)])  19.5 us
    dot_general x4, matrix products, along_planes(): jnp.einsum('zyx,zk->kyx', padded, matrix, precision=lax.Precision.HIGHEST)  15.4 us
    ppermute x10, starting transfers between devices, extended(): lax.ppermute(head, axis, [((i + 1) % count, i) for i in range(ends)])  12.9 us
    ppermute x10, waiting for transfers between devices, extended(): lax.ppermute(tail, axis, [(i, (i + 1) % count) for i in range(ends)])  11 us
    concatenate x6, other arithmetic, extended(): jnp.concatenate([lax.ppermute(tail, axis, [(i, (i + 1) % count) for i in...  9.65 us
    dot_general x4, matrix products, along_x(): jnp.einsum('zyx,xk->zyk', vol, matrix, precision=lax.Precision.HIGHEST)  7.28 us
  transfers between devices with their start and end apart: 22, of which 13 were waited for; matrix products, arithmetic and copies ran while one was open for 7% of the time, Pallas kernels for 0%

profile of v1, /device:TPU:0, one launch (start us, length us, event | category | flops | bytes accessed | tf_op | source)
XLA Modules:
  0.0 271.1 jit_solution(11250390171585052544)
XLA Ops:
  7.8 3.1 %collective-permute-start = (bf16[32,64,128]{2,1,0:T(8,128)(2,1)}, bf16[32,64,128]{2,1,0:T(8,128)(2,1)S(1)}, u32[]{:S(2)}, u32[]{:S(2)}) collective-permute-start(bf16[32,64,128]{2,1,0:T(8,128)(2,1)} %bitcast.61), channel_id=1, source_target_pairs={{0,1},{2,3},{4,5},{6,7},{8,9},{10,11},{12,13},{14,15},{16,17},{18,... | collective-permute-start | bytes 1572872 | tf_op jit(solution)/shard_map/ppermute | solution.py:19
  13.4 2.2 fusion.14
  17.0 6.3 %collective-permute-start.4 = (bf16[32,31,128]{2,1,0:T(8,128)(2,1)S(1)}, bf16[32,31,128]{2,1,0:T(8,128)(2,1)}, u32[]{:S(2)}, u32[]{:S(2)}) collective-permute-start(bf16[32,31,128]{2,1,0:T(8,128)(2,1)S(1)} %get-tuple-element.27), channel_id=1, source_target_pairs={{0,2},{2,4},{4,6},{1,3},{3,5},{5,7},{8,10},{10,12},{12,14},{9,11},... | collective-permute-start | bytes 761864 | tf_op jit(solution)/shard_map/ppermute | solution.py:19
  23.2 4.1 %iota_compare_fusion = (pred[96,128,192]{2,1,0:T(8,128)(4,1)}, pred[96,128,192]{2,1,0:T(8,128)(4,1)}) fusion(), kind=kLoop, calls=%fused_computation | loop fusion | flops 4718592 | bytes 4718592 | tf_op jit(solution)/shard_map/jit(_pad)/pad | solution.py:60
  32.7 5.1 %collective-permute-start.6 = (f32[31,64,128]{2,1,0:T(8,128)}, f32[31,64,128]{2,1,0:T(8,128)}, u32[]{:S(2)}, u32[]{:S(2)}) collective-permute-start(f32[31,64,128]{2,1,0:T(8,128)} %get-tuple-element.19), channel_id=1, source_target_pairs={{0,1},{2,3},{4,5},{6,7},{8,9},{10,11},{12,13},{14,15},{16,17},{18,... | collective-permute-start | bytes 3047432 | tf_op jit(solution)/shard_map/ppermute | solution.py:19
  46.0 4.9 %collective-permute-start.2 = (bf16[96,32,128]{2,1,0:T(8,128)(2,1)S(1)}, bf16[96,32,128]{2,1,0:T(8,128)(2,1)S(1)}, u32[]{:S(2)}, u32[]{:S(2)}) collective-permute-start(bf16[96,32,128]{2,1,0:T(8,128)(2,1)S(1)} %get-tuple-element.11), channel_id=1, source_target_pairs={{0,2},{2,4},{4,6},{1,3},{3,5},{5,7},{8,10},{10,12},{12,14},{9,11},... | collective-permute-start | bytes 2359304 | tf_op jit(solution)/shard_map/ppermute | solution.py:19
  53.1 3.4 %fusion.2 = f32[32,64,128]{2,0,1:T(8,128)S(1)} fusion(f32[94,64,128]{2,1,0:T(8,128)S(1)} %pad_maximum_fusion, f32[94,32]{0,1:T(8,128)S(1)} %get-tuple-element.10), kind=kOutput, calls=%fused_computation.12 | convolution fusion | flops 295698432 | bytes 4140800 | tf_op jit(solution)/shard_map/zyx,zk->kyx/dot_general | solution.py:49
  56.5 8.3 %collective-permute-done.3 = bf16[96,32,128]{2,1,0:T(8,128)(2,1)S(1)} collective-permute-done((bf16[96,32,128]{2,1,0:T(8,128)(2,1)S(1)}, bf16[96,32,128]{2,1,0:T(8,128)(2,1)S(1)}, u32[]{:S(2)}, u32[]{:S(2)}) %collective-permute-start.3) | collective-permute-done | bytes 786464 | tf_op jit(solution)/shard_map/ppermute | solution.py:21
  66.0 6.5 %fusion.48 = bf16[32,64,128]{2,1,0:T(8,128)(2,1)S(1)} fusion(s32[]{:T(128)S(6)} %select_n.61, s32[]{:T(128)S(6)} %select_n.62, s32[]{:T(128)S(6)} %select_n.63, bf16[96,32,128]{2,1,0:T(8,128)(2,1)S(1)} %collective-permute-done.3, bf16[96,32,128]{2,1,0:T(8,128)(2,1)S(1)} %collective-permute-done.2, bf16[32,64,128]{2,1,0:T(8,128)(2,1)S(1)} %collective-permute-done.1, ...), kind=kLoop, calls=%fused_computation.81 | loop fusion | flops 5242880 | bytes 4196352 | tf_op jit(solution)/shard_map/concatenate | solution.py:17
  75.6 5.2 %collective-permute-start.8 = (bf16[32,31,128]{2,1,0:T(8,128)(2,1)S(1)}, bf16[32,31,128]{2,1,0:T(8,128)(2,1)S(1)}, u32[]{:S(2)}, u32[]{:S(2)}) collective-permute-start(bf16[32,31,128]{2,1,0:T(8,128)(2,1)S(1)} %get-tuple-element.25), channel_id=1, source_target_pairs={{0,2},{2,4},{4,6},{1,3},{3,5},{5,7},{8,10},{10,12},{12,14},{9,11},... | collective-permute-start | bytes 761864 | tf_op jit(solution)/shard_map/ppermute | solution.py:19
  80.8 2.2 collective-permute-done.9
  88.1 3.2 %collective-permute-start.10 = (f32[31,64,128]{2,1,0:T(8,128)}, f32[31,64,128]{2,1,0:T(8,128)S(1)}, u32[]{:S(2)}, u32[]{:S(2)}) collective-permute-start(f32[31,64,128]{2,1,0:T(8,128)} %get-tuple-element.17), channel_id=1, source_target_pairs={{0,1},{2,3},{4,5},{6,7},{8,9},{10,11},{12,13},{14,15},{16,17},{18,... | collective-permute-start | bytes 3047432 | tf_op jit(solution)/shard_map/ppermute | solution.py:19
  94.0 4.3 %fusion.8 = f32[32,64,128]{2,0,1:T(8,128)} fusion(f32[94,64,128]{2,1,0:T(8,128)S(1)} %pad_maximum_fusion.1, f32[64,128]{1,0:T(8,128)S(1)} %dynamic-slice_bitcast_fusion, f32[94,32]{0,1:T(8,128)S(1)} %get-tuple-element.9), kind=kOutput, calls=%fused_computation.26 | convolution fusion | flops 295960576 | bytes 4173568 | tf_op jit(solution)/shard_map/zyx,zk->kyx/dot_general | solution.py:49
  98.4 55.6 %all-reduce.4.cloned.1.call-done = f32[32,64,128]{2,0,1:T(8,128)} async-done(((f32[32,64,128]{2,0,1:T(8,128)}), f32[32,64,128]{2,0,1:T(8,128)}) %all-reduce.4.cloned.1.call-update) | async-done | bytes 1048592 | tf_op jit(solution)/shard_map/psum | solution.py:94
  158.9 4.6 %collective-permute-start.12 = (bf16[32,31,128]{2,1,0:T(8,128)(2,1)S(1)}, bf16[32,31,128]{2,1,0:T(8,128)(2,1)S(1)}, u32[]{:S(2)}, u32[]{:S(2)}) collective-permute-start(bf16[32,31,128]{2,1,0:T(8,128)(2,1)S(1)} %get-tuple-element.23), channel_id=1, source_target_pairs={{0,2},{2,4},{4,6},{1,3},{3,5},{5,7},{8,10},{10,12},{12,14},{9,11},... | collective-permute-start | bytes 761864 | tf_op jit(solution)/shard_map/ppermute | solution.py:19
  163.5 4.1 %collective-permute-done.13 = bf16[32,31,128]{2,1,0:T(8,128)(2,1)S(1)} collective-permute-done((bf16[32,31,128]{2,1,0:T(8,128)(2,1)S(1)}, bf16[32,31,128]{2,1,0:T(8,128)(2,1)S(1)}, u32[]{:S(2)}, u32[]{:S(2)}) %collective-permute-start.13) | collective-permute-done | bytes 253984 | tf_op jit(solution)/shard_map/ppermute | solution.py:21
  171.0 3.4 %collective-permute-start.14 = (f32[31,64,128]{2,1,0:T(8,128)S(1)}, f32[31,64,128]{2,1,0:T(8,128)S(1)}, u32[]{:S(2)}, u32[]{:S(2)}) collective-permute-start(f32[31,64,128]{2,1,0:T(8,128)S(1)} %get-tuple-element.15), channel_id=1, source_target_pairs={{0,1},{2,3},{4,5},{6,7},{8,9},{10,11},{12,13},{14,15},{16,17},{18,... | collective-permute-start | bytes 3047432 | tf_op jit(solution)/shard_map/ppermute | solution.py:19
  176.8 3.4 %fusion = f32[32,64,128]{2,0,1:T(8,128)S(1)} fusion(f32[94,64,128]{2,1,0:T(8,128)S(1)} %pad_maximum_fusion.2, f32[94,32]{0,1:T(8,128)S(1)} %get-tuple-element.10), kind=kOutput, calls=%fused_computation.10 | convolution fusion | flops 295698432 | bytes 4140800 | tf_op jit(solution)/shard_map/zyx,zk->kyx/dot_general | solution.py:49
  183.3 5.0 %collective-permute-start.16 = (bf16[32,31,128]{2,1,0:T(8,128)(2,1)S(1)}, bf16[32,31,128]{2,1,0:T(8,128)(2,1)S(1)}, u32[]{:S(2)}, u32[]{:S(2)}) collective-permute-start(bf16[32,31,128]{2,1,0:T(8,128)(2,1)S(1)} %get-tuple-element.21), channel_id=1, source_target_pairs={{0,2},{2,4},{4,6},{1,3},{3,5},{5,7},{8,10},{10,12},{12,14},{9,11},... | collective-permute-start | bytes 761864 | tf_op jit(solution)/shard_map/ppermute | solution.py:19
  188.3 4.9 %collective-permute-done.17 = bf16[32,31,128]{2,1,0:T(8,128)(2,1)S(1)} collective-permute-done((bf16[32,31,128]{2,1,0:T(8,128)(2,1)S(1)}, bf16[32,31,128]{2,1,0:T(8,128)(2,1)S(1)}, u32[]{:S(2)}, u32[]{:S(2)}) %collective-permute-start.17) | collective-permute-done | bytes 253984 | tf_op jit(solution)/shard_map/ppermute | solution.py:21
  196.7 3.2 %collective-permute-start.18 = (f32[31,64,128]{2,1,0:T(8,128)S(1)}, f32[31,64,128]{2,1,0:T(8,128)S(1)}, u32[]{:S(2)}, u32[]{:S(2)}) collective-permute-start(f32[31,64,128]{2,1,0:T(8,128)S(1)} %get-tuple-element.13), channel_id=1, source_target_pairs={{0,1},{2,3},{4,5},{6,7},{8,9},{10,11},{12,13},{14,15},{16,17},{18,... | collective-permute-start | bytes 3047432 | tf_op jit(solution)/shard_map/ppermute | solution.py:19
  199.9 2.1 collective-permute-done.18
  202.4 4.3 %fusion.11 = f32[32,64,128]{2,0,1:T(8,128)} fusion(f32[94,64,128]{2,1,0:T(8,128)S(1)} %pad_maximum_fusion.3, f32[64,128]{1,0:T(8,128)S(1)} %dynamic-slice_bitcast_fusion, f32[94,32]{0,1:T(8,128)S(1)} %get-tuple-element.9), kind=kOutput, calls=%fused_computation.27 | convolution fusion | flops 295960576 | bytes 4173568 | tf_op jit(solution)/shard_map/zyx,zk->kyx/dot_general | solution.py:49
  206.7 54.0 %all-reduce.6.cloned.1.call-done = f32[32,64,128]{2,0,1:T(8,128)} async-done(((f32[32,64,128]{2,0,1:T(8,128)}), f32[32,64,128]{2,0,1:T(8,128)}) %all-reduce.6.cloned.1.call-update) | async-done | bytes 1048592 | tf_op jit(solution)/shard_map/psum | solution.py:94
  (85 shorter events, 47.8 us)
Async XLA Ops:
  6.5 147.4 %all-reduce.4.cloned.1.call-start = ((), (), s32[]{:S(2)}) async-start(), calls=%async_computation | async-start | bytes 2097152 | tf_op jit(solution)/shard_map/psum | solution.py:94
  6.5 37.6 %collective-permute-start.1 = (bf16[32,64,128]{2,1,0:T(8,128)(2,1)}, bf16[32,64,128]{2,1,0:T(8,128)(2,1)S(1)}, u32[]{:S(2)}, u32[]{:S(2)}) collective-permute-start(bf16[32,64,128]{2,1,0:T(8,128)(2,1)} %bitcast.60), channel_id=1, source_target_pairs={{1,0},{3,2},{5,4},{7,6},{9,8},{11,10},{13,12},{15,14},{17,16},{19,... | collective-permute-start | bytes 1572872 | tf_op jit(solution)/shard_map/ppermute | solution.py:21
  7.8 36.4 %collective-permute-start = (bf16[32,64,128]{2,1,0:T(8,128)(2,1)}, bf16[32,64,128]{2,1,0:T(8,128)(2,1)S(1)}, u32[]{:S(2)}, u32[]{:S(2)}) collective-permute-start(bf16[32,64,128]{2,1,0:T(8,128)(2,1)} %bitcast.61), channel_id=1, source_target_pairs={{0,1},{2,3},{4,5},{6,7},{8,9},{10,11},{12,13},{14,15},{16,17},{18,... | collective-permute-start | bytes 1572872 | tf_op jit(solution)/shard_map/ppermute | solution.py:19
  15.7 12.3 %collective-permute-start.5 = (bf16[32,31,128]{2,1,0:T(8,128)(2,1)S(1)}, bf16[32,31,128]{2,1,0:T(8,128)(2,1)}, u32[]{:S(2)}, u32[]{:S(2)}) collective-permute-start(bf16[32,31,128]{2,1,0:T(8,128)(2,1)S(1)} %get-tuple-element.28), channel_id=1, source_target_pairs={{2,0},{4,2},{6,4},{3,1},{5,3},{7,5},{10,8},{12,10},{14,12},{11,9},... | collective-permute-start | bytes 761864 | tf_op jit(solution)/shard_map/ppermute | solution.py:21
  17.0 11.0 %collective-permute-start.4 = (bf16[32,31,128]{2,1,0:T(8,128)(2,1)S(1)}, bf16[32,31,128]{2,1,0:T(8,128)(2,1)}, u32[]{:S(2)}, u32[]{:S(2)}) collective-permute-start(bf16[32,31,128]{2,1,0:T(8,128)(2,1)S(1)} %get-tuple-element.27), channel_id=1, source_target_pairs={{0,2},{2,4},{4,6},{1,3},{3,5},{5,7},{8,10},{10,12},{12,14},{9,11},... | collective-permute-start | bytes 761864 | tf_op jit(solution)/shard_map/ppermute | solution.py:19
  28.0 16.2 %copy-start.1 = (bf16[1,32,64,128]{3,2,1,0:T(8,128)(2,1)S(1)}, bf16[1,32,64,128]{3,2,1,0:T(8,128)(2,1)}, u32[]{:S(2)}) copy-start(bf16[1,32,64,128]{3,2,1,0:T(8,128)(2,1)} %param.6) | copy-start | bytes 1572868
  31.4 19.8 %collective-permute-start.7 = (f32[31,64,128]{2,1,0:T(8,128)}, f32[31,64,128]{2,1,0:T(8,128)}, u32[]{:S(2)}, u32[]{:S(2)}) collective-permute-start(f32[31,64,128]{2,1,0:T(8,128)} %get-tuple-element.20), channel_id=1, source_target_pairs={{1,0},{3,2},{5,4},{7,6},{9,8},{11,10},{13,12},{15,14},{17,16},{19,... | collective-permute-start | bytes 3047432 | tf_op jit(solution)/shard_map/ppermute | solution.py:21
  32.7 18.5 %collective-permute-start.6 = (f32[31,64,128]{2,1,0:T(8,128)}, f32[31,64,128]{2,1,0:T(8,128)}, u32[]{:S(2)}, u32[]{:S(2)}) collective-permute-start(f32[31,64,128]{2,1,0:T(8,128)} %get-tuple-element.19), channel_id=1, source_target_pairs={{0,1},{2,3},{4,5},{6,7},{8,9},{10,11},{12,13},{14,15},{16,17},{18,... | collective-permute-start | bytes 3047432 | tf_op jit(solution)/shard_map/ppermute | solution.py:19
  44.7 20.1 %collective-permute-start.3 = (bf16[96,32,128]{2,1,0:T(8,128)(2,1)S(1)}, bf16[96,32,128]{2,1,0:T(8,128)(2,1)S(1)}, u32[]{:S(2)}, u32[]{:S(2)}) collective-permute-start(bf16[96,32,128]{2,1,0:T(8,128)(2,1)S(1)} %get-tuple-element.12), channel_id=1, source_target_pairs={{2,0},{4,2},{6,4},{3,1},{5,3},{7,5},{10,8},{12,10},{14,12},{11,9},... | collective-permute-start | bytes 2359304 | tf_op jit(solution)/shard_map/ppermute | solution.py:21
  46.0 20.0 %collective-permute-start.2 = (bf16[96,32,128]{2,1,0:T(8,128)(2,1)S(1)}, bf16[96,32,128]{2,1,0:T(8,128)(2,1)S(1)}, u32[]{:S(2)}, u32[]{:S(2)}) collective-permute-start(bf16[96,32,128]{2,1,0:T(8,128)(2,1)S(1)} %get-tuple-element.11), channel_id=1, source_target_pairs={{0,2},{2,4},{4,6},{1,3},{3,5},{5,7},{8,10},{10,12},{12,14},{9,11},... | collective-permute-start | bytes 2359304 | tf_op jit(solution)/shard_map/ppermute | solution.py:19
  74.3 8.7 %collective-permute-start.9 = (bf16[32,31,128]{2,1,0:T(8,128)(2,1)S(1)}, bf16[32,31,128]{2,1,0:T(8,128)(2,1)S(1)}, u32[]{:S(2)}, u32[]{:S(2)}) collective-permute-start(bf16[32,31,128]{2,1,0:T(8,128)(2,1)S(1)} %get-tuple-element.26), channel_id=1, source_target_pairs={{2,0},{4,2},{6,4},{3,1},{5,3},{7,5},{10,8},{12,10},{14,12},{11,9},... | collective-permute-start | bytes 761864 | tf_op jit(solution)/shard_map/ppermute | solution.py:21
  75.6 8.9 %collective-permute-start.8 = (bf16[32,31,128]{2,1,0:T(8,128)(2,1)S(1)}, bf16[32,31,128]{2,1,0:T(8,128)(2,1)S(1)}, u32[]{:S(2)}, u32[]{:S(2)}) collective-permute-start(bf16[32,31,128]{2,1,0:T(8,128)(2,1)S(1)} %get-tuple-element.25), channel_id=1, source_target_pairs={{0,2},{2,4},{4,6},{1,3},{3,5},{5,7},{8,10},{10,12},{12,14},{9,11},... | collective-permute-start | bytes 761864 | tf_op jit(solution)/shard_map/ppermute | solution.py:19
  86.8 4.8 %collective-permute-start.11 = (f32[31,64,128]{2,1,0:T(8,128)}, f32[31,64,128]{2,1,0:T(8,128)S(1)}, u32[]{:S(2)}, u32[]{:S(2)}) collective-permute-start(f32[31,64,128]{2,1,0:T(8,128)} %get-tuple-element.18), channel_id=1, source_target_pairs={{1,0},{3,2},{5,4},{7,6},{9,8},{11,10},{13,12},{15,14},{17,16},{19,... | collective-permute-start | bytes 3047432 | tf_op jit(solution)/shard_map/ppermute | solution.py:21
  88.1 5.5 %collective-permute-start.10 = (f32[31,64,128]{2,1,0:T(8,128)}, f32[31,64,128]{2,1,0:T(8,128)S(1)}, u32[]{:S(2)}, u32[]{:S(2)}) collective-permute-start(f32[31,64,128]{2,1,0:T(8,128)} %get-tuple-element.17), channel_id=1, source_target_pairs={{0,1},{2,3},{4,5},{6,7},{8,9},{10,11},{12,13},{14,15},{16,17},{18,... | collective-permute-start | bytes 3047432 | tf_op jit(solution)/shard_map/ppermute | solution.py:19
  93.9 60.0 %copy-start = (f32[32,64,128]{2,1,0:T(8,128)S(1)}, f32[32,64,128]{2,1,0:T(8,128)}, u32[]{:S(2)}) copy-start(f32[32,64,128]{2,1,0:T(8,128)} %param.5) | copy-start | bytes 3145732
  98.3 162.4 %all-reduce.6.cloned.1.call-start = ((), (), s32[]{:S(2)}) async-start(), calls=%async_computation.1 | async-start | bytes 2097152 | tf_op jit(solution)/shard_map/psum | solution.py:94
  157.6 9.9 %collective-permute-start.13 = (bf16[32,31,128]{2,1,0:T(8,128)(2,1)S(1)}, bf16[32,31,128]{2,1,0:T(8,128)(2,1)S(1)}, u32[]{:S(2)}, u32[]{:S(2)}) collective-permute-start(bf16[32,31,128]{2,1,0:T(8,128)(2,1)S(1)} %get-tuple-element.24), channel_id=1, source_target_pairs={{2,0},{4,2},{6,4},{3,1},{5,3},{7,5},{10,8},{12,10},{14,12},{11,9},... | collective-permute-start | bytes 761864 | tf_op jit(solution)/shard_map/ppermute | solution.py:21
  158.9 9.8 %collective-permute-start.12 = (bf16[32,31,128]{2,1,0:T(8,128)(2,1)S(1)}, bf16[32,31,128]{2,1,0:T(8,128)(2,1)S(1)}, u32[]{:S(2)}, u32[]{:S(2)}) collective-permute-start(bf16[32,31,128]{2,1,0:T(8,128)(2,1)S(1)} %get-tuple-element.23), channel_id=1, source_target_pairs={{0,2},{2,4},{4,6},{1,3},{3,5},{5,7},{8,10},{10,12},{12,14},{9,11},... | collective-permute-start | bytes 761864 | tf_op jit(solution)/shard_map/ppermute | solution.py:19
  169.7 4.7 %collective-permute-start.15 = (f32[31,64,128]{2,1,0:T(8,128)S(1)}, f32[31,64,128]{2,1,0:T(8,128)S(1)}, u32[]{:S(2)}, u32[]{:S(2)}) collective-permute-start(f32[31,64,128]{2,1,0:T(8,128)S(1)} %get-tuple-element.16), channel_id=1, source_target_pairs={{1,0},{3,2},{5,4},{7,6},{9,8},{11,10},{13,12},{15,14},{17,16},{19,... | collective-permute-start | bytes 3047432 | tf_op jit(solution)/shard_map/ppermute | solution.py:21
  171.0 5.3 %collective-permute-start.14 = (f32[31,64,128]{2,1,0:T(8,128)S(1)}, f32[31,64,128]{2,1,0:T(8,128)S(1)}, u32[]{:S(2)}, u32[]{:S(2)}) collective-permute-start(f32[31,64,128]{2,1,0:T(8,128)S(1)} %get-tuple-element.15), channel_id=1, source_target_pairs={{0,1},{2,3},{4,5},{6,7},{8,9},{10,11},{12,13},{14,15},{16,17},{18,... | collective-permute-start | bytes 3047432 | tf_op jit(solution)/shard_map/ppermute | solution.py:19
  182.0 11.2 %collective-permute-start.17 = (bf16[32,31,128]{2,1,0:T(8,128)(2,1)S(1)}, bf16[32,31,128]{2,1,0:T(8,128)(2,1)S(1)}, u32[]{:S(2)}, u32[]{:S(2)}) collective-permute-start(bf16[32,31,128]{2,1,0:T(8,128)(2,1)S(1)} %get-tuple-element.22), channel_id=1, source_target_pairs={{2,0},{4,2},{6,4},{3,1},{5,3},{7,5},{10,8},{12,10},{14,12},{11,9},... | collective-permute-start | bytes 761864 | tf_op jit(solution)/shard_map/ppermute | solution.py:21
  183.3 11.1 %collective-permute-start.16 = (bf16[32,31,128]{2,1,0:T(8,128)(2,1)S(1)}, bf16[32,31,128]{2,1,0:T(8,128)(2,1)S(1)}, u32[]{:S(2)}, u32[]{:S(2)}) collective-permute-start(bf16[32,31,128]{2,1,0:T(8,128)(2,1)S(1)} %get-tuple-element.21), channel_id=1, source_target_pairs={{0,2},{2,4},{4,6},{1,3},{3,5},{5,7},{8,10},{10,12},{12,14},{9,11},... | collective-permute-start | bytes 761864 | tf_op jit(solution)/shard_map/ppermute | solution.py:19
  195.4 4.5 %collective-permute-start.19 = (f32[31,64,128]{2,1,0:T(8,128)S(1)}, f32[31,64,128]{2,1,0:T(8,128)S(1)}, u32[]{:S(2)}, u32[]{:S(2)}) collective-permute-start(f32[31,64,128]{2,1,0:T(8,128)S(1)} %get-tuple-element.14), channel_id=1, source_target_pairs={{1,0},{3,2},{5,4},{7,6},{9,8},{11,10},{13,12},{15,14},{17,16},{19,... | collective-permute-start | bytes 3047432 | tf_op jit(solution)/shard_map/ppermute | solution.py:21
  196.7 5.3 %collective-permute-start.18 = (f32[31,64,128]{2,1,0:T(8,128)S(1)}, f32[31,64,128]{2,1,0:T(8,128)S(1)}, u32[]{:S(2)}, u32[]{:S(2)}) collective-permute-start(f32[31,64,128]{2,1,0:T(8,128)S(1)} %get-tuple-element.13), channel_id=1, source_target_pairs={{0,1},{2,3},{4,5},{6,7},{8,9},{10,11},{12,13},{14,15},{16,17},{18,... | collective-permute-start | bytes 3047432 | tf_op jit(solution)/shard_map/ppermute | solution.py:19
  (4 other events, 32.7 us)
Sparse Core Ops, SparseCore 0:
  98.4 55.4 all-reduce.3
  206.9 53.8 all-reduce.5

commit v2 on v1

v2 whole, which is shorter than its diff:
```python
import functools

import jax
import jax.numpy as jnp
from jax import lax
from jax.experimental import pallas as pl
from jax.experimental.pallas import tpu as pltpu
from jax.sharding import PartitionSpec as P

BLOCK = 128
ITERS = 2
MESH = pl.DeviceIdType.MESH
F32 = jnp.float32
BF16 = jnp.bfloat16


def split(value):
    high = value.astype(BF16)
    return high, (value - high.astype(F32)).astype(BF16)


def dot(a, b):
    return jnp.dot(a, b, preferred_element_type=F32)


def band(kern, axis, forms):
    marks = []
    for rows, cols, sign, base in forms:
        row = lax.broadcasted_iota(jnp.int32, (rows, cols), 0)
        col = lax.broadcasted_iota(jnp.int32, (rows, cols), 1)
        marks.append(base + sign * (row - col))

    def add_tap(tap, carry):
        total, mats = carry
        value = kern[0, axis, tap]
        return total + value, tuple(
            mat + jnp.where(mark == tap, value, 0.0) for mat, mark in zip(mats, marks)
        )

    zeros = tuple(jnp.zeros(mark.shape, F32) for mark in marks)
    total, mats = lax.fori_loop(0, kern.shape[2], add_tap, (jnp.float32(0.0), zeros))
    return [mat / total for mat in mats]


def kernel(
    strips, cov, shifts, kern, est, views, out,
    fext, bext, vext, data, mid, back, mast, own, term, slots, fin,
    rmat, xfor, xback, zmat, send, recv, local,
):
    slab, strip, width = est.shape
    half = strip // 2
    planes = 2 * slab
    taps = kern.shape[2]
    reach = (taps - 1) // 2
    quarter = planes // 4
    group = 8
    v, s, g = lax.axis_index("view"), lax.axis_index("xy"), lax.axis_index("gz")
    va, vb = lax.div(v, 2), lax.rem(v, 2)
    q = 2 * s + g
    has_prev, has_next = q > 0, q < 2 * strips - 1

    def other_view(k):
        return lax.rem(va + k // 2, 2) * 2 + lax.rem(vb + k % 2, 2)

    sibling = (v, s, 1 - g)
    before = (v, lax.rem(s - 1 + g + strips, strips), 1 - g)
    after = (v, lax.rem(s + g, strips), 1 - g)
    strip_before = lax.rem(s - 1 + strips, strips)
    strip_after = lax.rem(s + 1, strips)

    barrier = pltpu.get_barrier_semaphore()

    def greet(device):
        pl.semaphore_signal(barrier, inc=1, device_id=device, device_id_type=MESH)

    greet(sibling)
    for k in range(1, 4):
        greet((other_view(k), s, g))
        greet((other_view(k), s, 1 - g))

    @pl.when(s > 0)
    def _():
        greet((v, strip_before, 0))
        greet((v, strip_before, 1))

    @pl.when(s < strips - 1)
    def _():
        greet((v, strip_after, 0))
        greet((v, strip_after, 1))

    def remote(src, dst, send_id, recv_id, device):
        return pltpu.make_async_remote_copy(
            src_ref=src, dst_ref=dst, send_sem=send.at[send_id], recv_sem=recv.at[recv_id],
            device_id=device, device_id_type=MESH,
        )

    mine = pl.ds(pl.multiple_of(slab * g, slab), slab)
    lay = pl.multiple_of(half - half * g, half)
    first = fext.at[0]

    def lay_plane(i, carry):
        first[slab * g + i, pl.ds(lay, strip), :] = est[i].astype(BF16)
        vext[slab * g + i, pl.ds(lay, strip), :] = views[0, i]
        return carry

    lax.fori_loop(0, slab, lay_plane, 0)

    @pl.when(q == 0)
    def _():
        vext[:, 0:half, :] = jnp.zeros((planes, half, width), BF16)
        for n in range(ITERS):
            fext[n, :, 0:half, :] = jnp.zeros((planes, half, width), BF16)
            bext[n, :, 0:half, :] = jnp.zeros((planes, half, width), BF16)

    @pl.when(q == 2 * strips - 1)
    def _():
        vext[:, 2 * half :, :] = jnp.zeros((planes, half, width), BF16)
        for n in range(ITERS):
            fext[n, :, 2 * half :, :] = jnp.zeros((planes, half, width), BF16)
            bext[n, :, 2 * half :, :] = jnp.zeros((planes, half, width), BF16)

    pl.semaphore_wait(
        barrier, 7 + 2 * (s > 0).astype(jnp.int32) + 2 * (s < strips - 1).astype(jnp.int32)
    )

    def spread(ext, base):
        src_rows = lay
        across = remote(
            ext.at[mine, pl.ds(lay, strip), :],
            ext.at[mine, pl.ds(pl.multiple_of(half * g, half), strip), :],
            base, base, sibling,
        )
        down = remote(
            ext.at[mine, pl.ds(src_rows, half), :], ext.at[mine, 2 * half : 3 * half, :],
            base + 1, base + 1 + g, (v, strip_before, 1),
        )
        up = remote(
            ext.at[mine, pl.ds(pl.multiple_of(src_rows + half, half), half), :],
            ext.at[mine, 0:half, :],
            base + 2, base + 1 + g, (v, strip_after, 0),
        )
        return across, down, up

    def spread_start(copies):
        across, down, up = copies

        @pl.when(s > 0)
        def _():
            down.start()

        @pl.when(s < strips - 1)
        def _():
            up.start()

        across.start()

    def spread_arrive(ext, base):
        theirs = pl.ds(pl.multiple_of(slab * (1 - g), slab), slab)
        remote(
            ext.at[mine, pl.ds(lay, strip), :], ext.at[theirs, pl.ds(lay, strip), :],
            base, base, sibling,
        ).wait_recv()
        for c in range(2):
            part = pl.ds(c * slab, slab)

            @pl.when(jnp.logical_and(g == 0, s > 0))
            def _():
                remote(
                    ext.at[part, half : 2 * half, :], ext.at[part, 0:half, :],
                    base, base + 1 + c, sibling,
                ).wait_recv()

            @pl.when(jnp.logical_and(g == 1, s < strips - 1))
            def _():
                remote(
                    ext.at[part, half : 2 * half, :], ext.at[part, 2 * half : 3 * half, :],
                    base, base + 1 + c, sibling,
                ).wait_recv()

    def spread_sent(copies):
        across, down, up = copies
        across.wait_send()

        @pl.when(s > 0)
        def _():
            down.wait_send()

        @pl.when(s < strips - 1)
        def _():
            up.wait_send()

    est_copies = spread(first, 0)
    spread_start(est_copies)
    view_copies = spread(vext, 3)
    spread_start(view_copies)
    quarter_here = pl.ds(pl.multiple_of(quarter * vb, quarter), quarter)
    mast_copy = remote(
        est.at[quarter_here, pl.ds(pl.multiple_of(half * (1 - g), half), half), :],
        mast, 6, 6, sibling,
    )

    @pl.when(g == va)
    def _():
        mast_copy.start()
        mast[...] = est[quarter_here, pl.ds(pl.multiple_of(half * g, half), half), :]

    x_forward, = band(kern, 2, [(width, width, 1, reach)])
    x_backward, = band(kern, 2, [(width, width, -1, reach)])
    high, low = split(x_forward)
    xfor[:, :width] = high
    xfor[:, width:] = low
    high, low = split(x_backward)
    xback[:width, :width] = high
    xback[:width, width:] = low
    xback[width:, :width] = high
    xback[width:, width:] = jnp.zeros((width, width), BF16)
    z_mats = band(kern, 0, [(planes, planes, -1, reach), (planes, planes, 1, reach)])
    r_mats = band(
        kern, 1, [(half, 3 * half, -1, reach - half), (half, 3 * half, 1, reach + half)]
    )
    for way in range(2):
        high, low = split(z_mats[way])
        zmat[way, :planes, :] = high
        zmat[way, planes:, :] = low
        high, low = split(r_mats[way])
        rmat[way, :half, :] = high
        rmat[way, half:, :] = low

    def halo(ext, base, k):
        part = pl.ds(pl.multiple_of(quarter * other_view(k), quarter), quarter)
        src = ext.at[part, half : 2 * half, :]
        return (
            remote(src, ext.at[part, 2 * half : 3 * half, :], base + 2 * k, base + 2 * k, before),
            remote(src, ext.at[part, 0:half, :], base + 2 * k + 1, base + 2 * k + 1, after),
        )

    def halo_start(copies):
        down, up = copies

        @pl.when(has_prev)
        def _():
            down.start()

        @pl.when(has_next)
        def _():
            up.start()

    def halo_arrive(copies):
        down, up = copies

        @pl.when(has_next)
        def _():
            down.wait_recv()

        @pl.when(has_prev)
        def _():
            up.wait_recv()

    def halo_sent(copies):
        down, up = copies

        @pl.when(has_prev)
        def _():
            down.wait_send()

        @pl.when(has_next)
        def _():
            up.wait_send()

    def along_rows(ext, way, plane, load=None):
        load = load or (lambda i: ext[plane + i])
        mat = rmat[way]
        parts = []
        for i in range(0, group, 2):
            both = dot(mat, jnp.concatenate([load(i), load(i + 1)], axis=1))
            both = both[:half] + both[half:]
            parts += [both[:, :width], both[:, width:]]
        return jnp.concatenate(parts, axis=0)

    def forward(ext, plane):
        both = dot(along_rows(ext, 0, plane).astype(BF16), xfor[...])
        mid[pl.ds(pl.multiple_of(plane * half, group * half), group * half), :] = (
            both[:, :width] + both[:, width:]
        )

    def backward(ext, plane):
        high, low = split(along_rows(ext, 1, plane))
        both = dot(jnp.concatenate([high, low], axis=1), xback[...])
        return both[:, :width] + both[:, width:]

    def loop(steps, body):
        def step(i, carry):
            body(i)
            return carry

        lax.fori_loop(0, steps, step, 0)

    block = lax.div(q * half, BLOCK)
    weight = cov[v, block, 0].astype(F32)
    count = jnp.float32(0.0)
    for n in range(4):
        count = count + cov[n, block, 0].astype(F32)

    spread_arrive(first, 0)
    loop(planes // group, lambda i: forward(first, group * i))

    spread_arrive(vext, 3)
    row = lax.broadcasted_iota(jnp.int32, (half, 3 * half), 0)
    col = lax.broadcasted_iota(jnp.int32, (half, 3 * half), 1)
    pick_rows = (col == row + half + shifts[0, 1]).astype(F32).astype(BF16)
    row = lax.broadcasted_iota(jnp.int32, (width, width), 0)
    col = lax.broadcasted_iota(jnp.int32, (width, width), 1)
    pick_x = (row == col + shifts[0, 2]).astype(F32).astype(BF16)

    def window(i):
        parts = []
        for j in range(0, group, 2):
            pair, masks = [], []
            for n in range(2):
                plane = group * i + j + n + shifts[0, 0]
                inside = jnp.logical_and(plane >= 0, plane < planes)
                masks.append(inside.astype(jnp.int32).astype(F32))
                pair.append(vext[jnp.clip(plane, 0, planes - 1)])
            both = dot(pick_rows, jnp.concatenate(pair, axis=1))
            parts += [both[:, :width] * masks[0], both[:, width:] * masks[1]]
        moved = dot(jnp.concatenate(parts, axis=0).astype(BF16), pick_x)
        data[pl.ds(pl.multiple_of(group * half * i, group * half), group * half), :] = moved

    loop(planes // group, window)

    def column(ref, y):
        return jnp.concatenate(
            [ref[pl.ds(y, planes, stride=half), :], ref[pl.ds(y + 1, planes, stride=half), :]],
            axis=1,
        )

    def along_planes(i):
        for j in range(0, 4, 2):
            y = 4 * i + j
            both = dot(zmat[0], column(mid, y).astype(BF16))
            predicted = both[:planes] + both[planes:]
            ratio = column(data, y) / (predicted + 0.05)
            both = dot(zmat[1], ratio.astype(BF16))
            both = both[:planes] + both[planes:]
            back[pl.ds(y, planes, stride=half), :] = both[:, :width]
            back[pl.ds(y + 1, planes, stride=half), :] = both[:, width:]

    quarter_rows = quarter * half
    halos, terms, gathers = [], [], []
    for step in range(ITERS):
        loop(half // 4, along_planes)
        ext = bext.at[step]
        copies = {}
        for k in (3, 1, 2, 0):
            start = quarter * other_view(k)

            def lay_back(i):
                at = pl.multiple_of((start + i) * half, half)
                ext[start + i, half : 2 * half, :] = back[pl.ds(at, half), :].astype(BF16)

            loop(quarter, lay_back)
            copies[k] = halo(ext, 7 + 16 * step, k)
            halo_start(copies[k])
        for k in (3, 1, 2, 0):
            halo_arrive(copies[k])
            start = quarter * other_view(k)
            dest = own if k == 0 else term.at[step, k - 1]

            def correct(i):
                at = pl.multiple_of(group * half * i, group * half)
                dest[pl.ds(at, group * half), :] = weight * backward(ext, start + group * i)

            loop(quarter // group, correct)
            if k:
                sent = remote(
                    dest, slots.at[step, k - 1], 31 + 3 * step + k - 1, 31 + 3 * step + k - 1,
                    (other_view(k), s, g),
                )
                sent.start()
                terms.append(sent)
        halos += list(copies.values())
        if step == 0:

            @pl.when(g != va)
            def _():
                mast_copy.wait_recv()

        for sent in terms[-3:]:
            sent.wait_recv()
        last = step == ITERS - 1
        here = quarter * v

        def update(i):
            rows = pl.ds(pl.multiple_of(i * half, half), half)
            total = own[rows, :]
            for k in range(3):
                total = total + slots[step, k, rows, :]
            field = mast[i] * total / count
            if last:
                fin[i] = field
            else:
                mast[i] = field
                fext[step + 1, here + i, half : 2 * half, :] = field.astype(BF16)

        loop(quarter, update)
        if last:
            break
        ext = fext.at[step + 1]
        part = ext.at[pl.ds(pl.multiple_of(here, quarter), quarter), half : 2 * half, :]
        news = []
        for k in (3, 1, 2):
            sent = remote(part, part, 37 + k - 1, 37 + k - 1, (other_view(k), s, g))
            sent.start()
            news.append((k, sent))
        copies = [halo(ext, 47, k) for k in range(4)]
        halo_start(copies[0])
        for k in (1, 2, 3):
            theirs = ext.at[
                pl.ds(pl.multiple_of(quarter * other_view(k), quarter), quarter),
                half : 2 * half, :,
            ]
            remote(theirs, theirs, 37 + k - 1, 37 + k - 1, sibling).wait_recv()
            halo_start(copies[k])
        for k in range(4):
            halo_arrive(copies[k])
            start = quarter * other_view(k)
            loop(quarter // group, lambda i: forward(ext, start + group * i))
        halos += copies
        gathers += [sent for _, sent in news]

    place = out.at[
        quarter_here, pl.ds(pl.multiple_of(half * g, half), half), :
    ]
    arrive = 40 + 2 * vb + g
    results = [remote(fin, place, 40 + k, arrive, (other_view(k), s, va)) for k in range(4)]
    keep = pltpu.make_async_copy(fin, place, local.at[0])
    for k in (3, 1, 2):
        results[k].start()

    @pl.when(g == va)
    def _():
        keep.start()

    @pl.when(g != va)
    def _():
        results[0].start()

    for a in range(2):
        for b in range(2):
            spot = out.at[quarter * a : quarter * (a + 1), half * b : half * (b + 1), :]

            @pl.when(jnp.logical_or(v != 2 * g + a, g != b))
            def _():
                remote(fin, spot, 40, 40 + 2 * a + b, sibling).wait_recv()

    @pl.when(g == va)
    def _():
        keep.wait()
        mast_copy.wait_send()

    @pl.when(g != va)
    def _():
        results[0].wait_send()

    for k in (1, 2, 3):
        results[k].wait_send()
    spread_sent(est_copies)
    spread_sent(view_copies)
    for copies in halos:
        halo_sent(copies)
    for sent in terms + gathers:
        sent.wait_send()


def on_device(strips, estimate, views, shifts, kernels, coverage):
    slab, strip, width = estimate.shape
    half, planes = strip // 2, 2 * slab
    quarter = planes // 4
    vmem = pl.BlockSpec(memory_space=pltpu.VMEM)
    smem = pl.BlockSpec(memory_space=pltpu.SMEM)
    rows = planes * half
    scratch = [
        pltpu.VMEM((ITERS, planes, 3 * half, width), BF16),
        pltpu.VMEM((ITERS, planes, 3 * half, width), BF16),
        pltpu.VMEM((planes, 3 * half, width), BF16),
        pltpu.VMEM((rows, width), F32),
        pltpu.VMEM((rows, width), F32),
        pltpu.VMEM((rows, width), F32),
        pltpu.VMEM((quarter, half, width), F32),
        pltpu.VMEM((quarter * half, width), F32),
        pltpu.VMEM((ITERS, 3, quarter * half, width), F32),
        pltpu.VMEM((ITERS, 3, quarter * half, width), F32),
        pltpu.VMEM((quarter, half, width), F32),
        pltpu.VMEM((2, 2 * half, 3 * half), BF16),
        pltpu.VMEM((width, 2 * width), BF16),
        pltpu.VMEM((2 * width, 2 * width), BF16),
        pltpu.VMEM((2, 2 * planes, planes), BF16),
        pltpu.SemaphoreType.DMA((56,)),
        pltpu.SemaphoreType.DMA((56,)),
        pltpu.SemaphoreType.DMA((1,)),
    ]
    return pl.pallas_call(
        functools.partial(kernel, strips),
        out_shape=jax.ShapeDtypeStruct(estimate.shape, F32),
        in_specs=[smem, smem, smem, vmem, vmem],
        out_specs=pl.BlockSpec(memory_space=pl.ANY),
        scratch_shapes=scratch,
        compiler_params=pltpu.CompilerParams(
            collective_id=0, has_side_effects=True, vmem_limit_bytes=40 * 1024 * 1024
        ),
        cost_estimate=pl.CostEstimate(
            flops=12 * 2 * rows * width * 100, bytes_accessed=8 * rows * width, transcendentals=0
        ),
    )(coverage, shifts, kernels, estimate, views)


def solution(mesh):
    placed = (
        P("gz", "xy", None),
        P("view", "gz", "xy", None),
        P("view", None),
        P("view", None, None),
        P(),
    )
    return jax.shard_map(
        functools.partial(on_device, mesh.shape["xy"]),
        mesh=mesh, in_specs=placed, out_specs=P("gz", "xy", None), check_vma=False,
    )
```

time: 276 us -> 95.6 us (0.35)
  the two profiles are of different devices: /device:TPU:0 before, /device:TPU:9 now
where the time goes in v2:
time: 95.6 us; the launch traced here: 95.4 us
  Pallas kernels  90.8 us (95%)
  local copies, waits for them, and re-layouts  4.59 us (5%)
    pallas_call x1, Pallas kernels, on_device(): pl.pallas_call(functools.partial(kernel, strips), out_shape=jax.ShapeDtyp...  90.8 us
    unnamed x11, local copies, waits for them, and re-layouts  4.59 us

profile of v2, /device:TPU:9, one launch (start us, length us, event | category | flops | bytes accessed | tf_op | source)
XLA Modules:
  0.0 95.4 jit_solution(10953563346415918077)
XLA Ops:
  0.0 0.0 copy-start.3
  0.0 0.7 copy.7.kern
  0.7 0.0 copy-done.3
  0.7 0.0 copy-start.2
  0.7 0.1 copy.6.cov
  0.8 0.6 copy-done.2
  1.4 0.0 copy-start
  1.4 1.2 %copy-done = f32[32,64,128]{2,1,0:T(8,128)S(1)} copy-done((f32[32,64,128]{2,1,0:T(8,128)S(1)}, f32[32,64,128]{2,1,0:T(8,128)}, u32[]{:S(2)}) %copy-start) | copy-done | bytes 1048600
  2.6 0.0 copy-start.1
  2.6 1.0 %copy-done.1 = bf16[1,32,64,128]{3,2,1,0:T(8,128)(2,1)S(1)} copy-done((bf16[1,32,64,128]{3,2,1,0:T(8,128)(2,1)S(1)}, bf16[1,32,64,128]{3,2,1,0:T(8,128)(2,1)}, u32[]{:S(2)}) %copy-start.1) | copy-done | bytes 524312
  3.6 90.8 %shard_map.55 = f32[32,64,128]{2,1,0:T(8,128)S(1)} custom-call(s32[4,2,1]{2,1,0:T(2,128)S(1)} %copy.6.cov, s32[1,3]{1,0:T(1,128)S(1)} %copy-done.2, f32[1,3,63]{2,1,0:T(4,128)S(1)} %copy.7.kern, f32[32,64,128]{2,1,0:T(8,128)S(1)} %copy-done, bf16[1,32,64,128]{3,2,1,0:T(8,128)(2,1)S(1)} %copy-done.1), custom_call_target="tpu_custom_call" | custom-call | flops 629145600 | bytes 2097152 | tf_op jit(solution)/shard_map/pallas_call | solution.py:502
  94.4 1.0 %copy.9 = f32[32,64,128]{2,1,0:T(8,128)} copy(f32[32,64,128]{2,1,0:T(8,128)S(1)} %shard_map.55) | data formatting | bytes 2097152
Async XLA Ops:
  0.0 0.7 copy-start.3
  0.7 0.7 copy-start.2
  1.4 1.2 %copy-start = (f32[32,64,128]{2,1,0:T(8,128)S(1)}, f32[32,64,128]{2,1,0:T(8,128)}, u32[]{:S(2)}) copy-start(f32[32,64,128]{2,1,0:T(8,128)} %est.1) | copy-start | bytes 3145732
  2.6 1.0 %copy-start.1 = (bf16[1,32,64,128]{3,2,1,0:T(8,128)(2,1)S(1)}, bf16[1,32,64,128]{3,2,1,0:T(8,128)(2,1)}, u32[]{:S(2)}) copy-start(bf16[1,32,64,128]{3,2,1,0:T(8,128)(2,1)} %views.1) | copy-start | bytes 1572868

commit v3 on v2

--- a/solution.py
+++ b/solution.py
@@ -43,8 +43,8 @@
 
 
 def kernel(
-    strips, cov, shifts, kern, est, views, out,
-    fext, bext, vext, data, mid, back, mast, own, term, slots, fin,
+    strips, cov, shifts, kern, given, views, out,
+    est, fext, bext, vext, data, mid, back, mast, own, term, slots, fin,
     rmat, xfor, xback, zmat, send, recv, local,
 ):
     slab, strip, width = est.shape
@@ -62,6 +62,8 @@
     def other_view(k):
         return lax.rem(va + k // 2, 2) * 2 + lax.rem(vb + k % 2, 2)
 
+    fetch = pltpu.make_async_copy(given, est, local.at[0])
+    fetch.start()
     sibling = (v, s, 1 - g)
     before = (v, lax.rem(s - 1 + g + strips, strips), 1 - g)
     after = (v, lax.rem(s + g, strips), 1 - g)
@@ -98,12 +100,10 @@
     lay = pl.multiple_of(half - half * g, half)
     first = fext.at[0]
 
-    def lay_plane(i, carry):
-        first[slab * g + i, pl.ds(lay, strip), :] = est[i].astype(BF16)
-        vext[slab * g + i, pl.ds(lay, strip), :] = views[0, i]
-        return carry
-
-    lax.fori_loop(0, slab, lay_plane, 0)
+    lay_views = pltpu.make_async_copy(
+        views.at[0], vext.at[mine, pl.ds(lay, strip), :], local.at[1]
+    )
+    lay_views.start()
 
     @pl.when(q == 0)
     def _():
@@ -119,24 +119,26 @@
             fext[n, :, 2 * half :, :] = jnp.zeros((planes, half, width), BF16)
             bext[n, :, 2 * half :, :] = jnp.zeros((planes, half, width), BF16)
 
+    fetch.wait()
+    for i in range(0, slab, group):
+        first[pl.ds(slab * g + i, group), pl.ds(lay, strip), :] = est[i : i + group].astype(BF16)
+
     pl.semaphore_wait(
         barrier, 7 + 2 * (s > 0).astype(jnp.int32) + 2 * (s < strips - 1).astype(jnp.int32)
     )
 
-    def spread(ext, base):
-        src_rows = lay
+    def spread(ext, base, block):
         across = remote(
-            ext.at[mine, pl.ds(lay, strip), :],
+            block,
             ext.at[mine, pl.ds(pl.multiple_of(half * g, half), strip), :],
             base, base, sibling,
         )
         down = remote(
-            ext.at[mine, pl.ds(src_rows, half), :], ext.at[mine, 2 * half : 3 * half, :],
+            block.at[:, 0:half, :], ext.at[mine, 2 * half : 3 * half, :],
             base + 1, base + 1 + g, (v, strip_before, 1),
         )
         up = remote(
-            ext.at[mine, pl.ds(pl.multiple_of(src_rows + half, half), half), :],
-            ext.at[mine, 0:half, :],
+            block.at[:, half:strip, :], ext.at[mine, 0:half, :],
             base + 2, base + 1 + g, (v, strip_after, 0),
         )
         return across, down, up
@@ -189,10 +191,9 @@
         def _():
             up.wait_send()
 
-    est_copies = spread(first, 0)
+    est_copies = spread(first, 0, first.at[mine, pl.ds(lay, strip), :])
     spread_start(est_copies)
-    view_copies = spread(vext, 3)
-    spread_start(view_copies)
+    view_copies = spread(vext, 3, views.at[0])
     quarter_here = pl.ds(pl.multiple_of(quarter * vb, quarter), quarter)
     mast_copy = remote(
         est.at[quarter_here, pl.ds(pl.multiple_of(half * (1 - g), half), half), :],
@@ -288,12 +289,13 @@
         both = dot(jnp.concatenate([high, low], axis=1), xback[...])
         return both[:, :width] + both[:, width:]
 
-    def loop(steps, body):
+    def loop(steps, body, wide=1):
         def step(i, carry):
-            body(i)
+            for n in range(wide):
+                body(wide * i + n)
             return carry
 
-        lax.fori_loop(0, steps, step, 0)
+        lax.fori_loop(0, steps // wide, step, 0)
 
     block = lax.div(q * half, BLOCK)
     weight = cov[v, block, 0].astype(F32)
@@ -302,8 +304,10 @@
         count = count + cov[n, block, 0].astype(F32)
 
     spread_arrive(first, 0)
-    loop(planes // group, lambda i: forward(first, group * i))
-
+    spread_start(view_copies)
+    loop(planes // group, lambda i: forward(first, group * i), 2)
+
+    lay_views.wait()
     spread_arrive(vext, 3)
     row = lax.broadcasted_iota(jnp.int32, (half, 3 * half), 0)
     col = lax.broadcasted_iota(jnp.int32, (half, 3 * half), 1)
@@ -326,7 +330,7 @@
         moved = dot(jnp.concatenate(parts, axis=0).astype(BF16), pick_x)
         data[pl.ds(pl.multiple_of(group * half * i, group * half), group * half), :] = moved
 
-    loop(planes // group, window)
+    loop(planes // group, window, 2)
 
     def column(ref, y):
         return jnp.concatenate(
@@ -348,17 +352,16 @@
     quarter_rows = quarter * half
     halos, terms, gathers = [], [], []
     for step in range(ITERS):
-        loop(half // 4, along_planes)
+        loop(half // 4, along_planes, 2)
         ext = bext.at[step]
         copies = {}
         for k in (3, 1, 2, 0):
             start = quarter * other_view(k)
 
-            def lay_back(i):
-                at = pl.multiple_of((start + i) * half, half)
-                ext[start + i, half : 2 * half, :] = back[pl.ds(at, half), :].astype(BF16)
-
-            loop(quarter, lay_back)
+            at = pl.multiple_of(start * half, quarter * half)
+            ext[pl.ds(start, quarter), half : 2 * half, :] = (
+                back[pl.ds(at, quarter * half), :].reshape(quarter, half, width).astype(BF16)
+            )
             copies[k] = halo(ext, 7 + 16 * step, k)
             halo_start(copies[k])
         for k in (3, 1, 2, 0):
@@ -370,7 +373,7 @@
                 at = pl.multiple_of(group * half * i, group * half)
                 dest[pl.ds(at, group * half), :] = weight * backward(ext, start + group * i)
 
-            loop(quarter // group, correct)
+            loop(quarter // group, correct, 2)
             if k:
                 sent = remote(
                     dest, slots.at[step, k - 1], 31 + 3 * step + k - 1, 31 + 3 * step + k - 1,
@@ -391,18 +394,21 @@
         here = quarter * v
 
         def update(i):
-            rows = pl.ds(pl.multiple_of(i * half, half), half)
+            rows = pl.ds(pl.multiple_of(i * group * half, group * half), group * half)
             total = own[rows, :]
             for k in range(3):
                 total = total + slots[step, k, rows, :]
-            field = mast[i] * total / count
+            at = pl.ds(pl.multiple_of(i * group, group), group)
+            field = mast[at] * total.reshape(group, half, width) / count
             if last:
-                fin[i] = field
+                fin[at] = field
             else:
-                mast[i] = field
-                fext[step + 1, here + i, half : 2 * half, :] = field.astype(BF16)
-
-        loop(quarter, update)
+                mast[at] = field
+                fext[step + 1, pl.ds(here + i * group, group), half : 2 * half, :] = field.astype(
+                    BF16
+                )
+
+        loop(quarter // group, update)
         if last:
             break
         ext = fext.at[step + 1]
@@ -424,7 +430,7 @@
         for k in range(4):
             halo_arrive(copies[k])
             start = quarter * other_view(k)
-            loop(quarter // group, lambda i: forward(ext, start + group * i))
+            loop(quarter // group, lambda i: forward(ext, start + group * i), 2)
         halos += copies
         gathers += [sent for _, sent in news]
 
@@ -476,10 +482,11 @@
     slab, strip, width = estimate.shape
     half, planes = strip // 2, 2 * slab
     quarter = planes // 4
-    vmem = pl.BlockSpec(memory_space=pltpu.VMEM)
+    hbm = pl.BlockSpec(memory_space=pl.ANY)
     smem = pl.BlockSpec(memory_space=pltpu.SMEM)
     rows = planes * half
     scratch = [
+        pltpu.VMEM(estimate.shape, F32),
         pltpu.VMEM((ITERS, planes, 3 * half, width), BF16),
         pltpu.VMEM((ITERS, planes, 3 * half, width), BF16),
         pltpu.VMEM((planes, 3 * half, width), BF16),
@@ -497,13 +504,13 @@
         pltpu.VMEM((2, 2 * planes, planes), BF16),
         pltpu.SemaphoreType.DMA((56,)),
         pltpu.SemaphoreType.DMA((56,)),
-        pltpu.SemaphoreType.DMA((1,)),
+        pltpu.SemaphoreType.DMA((2,)),
     ]
     return pl.pallas_call(
         functools.partial(kernel, strips),
         out_shape=jax.ShapeDtypeStruct(estimate.shape, F32),
-        in_specs=[smem, smem, smem, vmem, vmem],
-        out_specs=pl.BlockSpec(memory_space=pl.ANY),
+        in_specs=[smem, smem, smem, hbm, hbm],
+        out_specs=hbm,
         scratch_shapes=scratch,
         compiler_params=pltpu.CompilerParams(
             collective_id=0, has_side_effects=True, vmem_limit_bytes=40 * 1024 * 1024

time: 95.6 us -> 93.5 us (0.978)
  Pallas kernels: 90.8 us -> 88.7 us
    pallas_call x1, Pallas kernels: 90.8 us -> 88.7 us  [on_device(): pl.pallas_call(functools.partial(kernel, strips), out_shape=jax.ShapeDtyp...]
where the time goes in v3:
time: 93.5 us; the launch traced here: 93.3 us
  Pallas kernels  88.7 us (95%)
  local copies, waits for them, and re-layouts  4.59 us (5%)
    pallas_call x1, Pallas kernels, on_device(): pl.pallas_call(functools.partial(kernel, strips), out_shape=jax.ShapeDtyp...  88.7 us
    unnamed x11, local copies, waits for them, and re-layouts  4.59 us

profile of v3, /device:TPU:9, one launch (start us, length us, event | category | flops | bytes accessed | tf_op | source)
XLA Modules:
  0.0 93.3 jit_solution(18006020281278460095)
XLA Ops:
  0.0 0.0 copy-start.3
  0.0 0.7 copy.7.kern
  0.7 0.0 copy-done.3
  0.7 0.0 copy-start.2
  0.7 0.1 copy.6.cov
  0.8 0.6 copy-done.2
  1.4 0.0 copy-start
  1.4 1.2 %copy-done = f32[32,64,128]{2,1,0:T(8,128)S(1)} copy-done((f32[32,64,128]{2,1,0:T(8,128)S(1)}, f32[32,64,128]{2,1,0:T(8,128)}, u32[]{:S(2)}) %copy-start) | copy-done | bytes 1048600
  2.6 0.0 copy-start.1
  2.6 1.0 %copy-done.1 = bf16[1,32,64,128]{3,2,1,0:T(8,128)(2,1)S(1)} copy-done((bf16[1,32,64,128]{3,2,1,0:T(8,128)(2,1)S(1)}, bf16[1,32,64,128]{3,2,1,0:T(8,128)(2,1)}, u32[]{:S(2)}) %copy-start.1) | copy-done | bytes 524312
  3.6 88.7 %shard_map.55 = f32[32,64,128]{2,1,0:T(8,128)S(1)} custom-call(s32[4,2,1]{2,1,0:T(2,128)S(1)} %copy.6.cov, s32[1,3]{1,0:T(1,128)S(1)} %copy-done.2, f32[1,3,63]{2,1,0:T(4,128)S(1)} %copy.7.kern, f32[32,64,128]{2,1,0:T(8,128)S(1)} %copy-done, bf16[1,32,64,128]{3,2,1,0:T(8,128)(2,1)S(1)} %copy-done.1), custom_call_target="tpu_custom_call" | custom-call | flops 629145600 | bytes 2097152 | tf_op jit(solution)/shard_map/pallas_call | solution.py:509
  92.3 1.0 %copy.9 = f32[32,64,128]{2,1,0:T(8,128)} copy(f32[32,64,128]{2,1,0:T(8,128)S(1)} %shard_map.55) | data formatting | bytes 2097152
Async XLA Ops:
  0.0 0.7 copy-start.3
  0.7 0.7 copy-start.2
  1.4 1.2 %copy-start = (f32[32,64,128]{2,1,0:T(8,128)S(1)}, f32[32,64,128]{2,1,0:T(8,128)}, u32[]{:S(2)}) copy-start(f32[32,64,128]{2,1,0:T(8,128)} %given.1) | copy-start | bytes 3145732
  2.6 1.0 %copy-start.1 = (bf16[1,32,64,128]{3,2,1,0:T(8,128)(2,1)S(1)}, bf16[1,32,64,128]{3,2,1,0:T(8,128)(2,1)}, u32[]{:S(2)}) copy-start(bf16[1,32,64,128]{3,2,1,0:T(8,128)(2,1)} %views.1) | copy-start | bytes 1572868

commit v4 on v3

v4 whole, which is shorter than its diff:
```python
import functools

import jax
import jax.numpy as jnp
from jax import lax
from jax.experimental import pallas as pl
from jax.experimental.pallas import tpu as pltpu
from jax.sharding import PartitionSpec as P

BLOCK = 128
ITERS = 2
MESH = pl.DeviceIdType.MESH
F32 = jnp.float32
BF16 = jnp.bfloat16


def split(value):
    high = value.astype(BF16)
    return high, (value - high.astype(F32)).astype(BF16)


def dot(a, b):
    return jnp.dot(a, b, preferred_element_type=F32)


def band(kern, axis, forms):
    marks = []
    for rows, cols, sign, base in forms:
        row = lax.broadcasted_iota(jnp.int32, (rows, cols), 0)
        col = lax.broadcasted_iota(jnp.int32, (rows, cols), 1)
        marks.append(base + sign * (row - col))

    def add_tap(tap, carry):
        total, mats = carry
        value = kern[0, axis, tap]
        return total + value, tuple(
            mat + jnp.where(mark == tap, value, 0.0) for mat, mark in zip(mats, marks)
        )

    zeros = tuple(jnp.zeros(mark.shape, F32) for mark in marks)
    total, mats = lax.fori_loop(0, kern.shape[2], add_tap, (jnp.float32(0.0), zeros))
    return [mat / total for mat in mats]


def kernel(
    strips, cov, shifts, kern, given, views, out,
    est, fext, bext, vext, data, mid, back, mast, own, term, slots, relay, fin,
    rmat, xfor, xback, zmat, send, recv, local,
):
    slab, strip, width = est.shape
    half = strip // 2
    planes = 2 * slab
    taps = kern.shape[2]
    reach = (taps - 1) // 2
    quarter = planes // 4
    group = quarter // 2
    v, s, g = lax.axis_index("view"), lax.axis_index("xy"), lax.axis_index("gz")
    va, vb = lax.div(v, 2), lax.rem(v, 2)
    q = 2 * s + g
    has_prev, has_next = q > 0, q < 2 * strips - 1

    def other_view(k):
        return lax.rem(va + k // 2, 2) * 2 + lax.rem(vb + k % 2, 2)

    fetch = pltpu.make_async_copy(given, est, local.at[0])
    fetch.start()
    sibling = (v, s, 1 - g)
    before = (v, lax.rem(s - 1 + g + strips, strips), 1 - g)
    after = (v, lax.rem(s + g, strips), 1 - g)
    strip_before = lax.rem(s - 1 + strips, strips)
    strip_after = lax.rem(s + 1, strips)

    barrier = pltpu.get_barrier_semaphore()

    def greet(device):
        pl.semaphore_signal(barrier, inc=1, device_id=device, device_id_type=MESH)

    greet(sibling)
    for k in range(1, 4):
        greet((other_view(k), s, g))
        greet((other_view(k), s, 1 - g))

    @pl.when(s > 0)
    def _():
        greet((v, strip_before, 0))
        greet((v, strip_before, 1))

    @pl.when(s < strips - 1)
    def _():
        greet((v, strip_after, 0))
        greet((v, strip_after, 1))

    def remote(src, dst, send_id, recv_id, device):
        return pltpu.make_async_remote_copy(
            src_ref=src, dst_ref=dst, send_sem=send.at[send_id], recv_sem=recv.at[recv_id],
            device_id=device, device_id_type=MESH,
        )

    mine = pl.ds(pl.multiple_of(slab * g, slab), slab)
    lay = pl.multiple_of(half - half * g, half)
    first = fext.at[0]

    lay_views = pltpu.make_async_copy(
        views.at[0], vext.at[mine, pl.ds(lay, strip), :], local.at[1]
    )
    lay_views.start()

    @pl.when(q == 0)
    def _():
        vext[:, 0:half, :] = jnp.zeros((planes, half, width), BF16)
        for n in range(ITERS):
            fext[n, :, 0:half, :] = jnp.zeros((planes, half, width), BF16)
            bext[n, :, 0:half, :] = jnp.zeros((planes, half, width), BF16)

    @pl.when(q == 2 * strips - 1)
    def _():
        vext[:, 2 * half :, :] = jnp.zeros((planes, half, width), BF16)
        for n in range(ITERS):
            fext[n, :, 2 * half :, :] = jnp.zeros((planes, half, width), BF16)
            bext[n, :, 2 * half :, :] = jnp.zeros((planes, half, width), BF16)

    fetch.wait()
    for i in range(0, slab, group):
        first[pl.ds(slab * g + i, group), pl.ds(lay, strip), :] = est[i : i + group].astype(BF16)

    pl.semaphore_wait(
        barrier, 7 + 2 * (s > 0).astype(jnp.int32) + 2 * (s < strips - 1).astype(jnp.int32)
    )

    def spread(ext, base, block):
        across = remote(
            block,
            ext.at[mine, pl.ds(pl.multiple_of(half * g, half), strip), :],
            base, base, sibling,
        )
        down, up = [], []
        for j in range(2):
            src = block.at[quarter * j : quarter * (j + 1)]
            part = pl.ds(pl.multiple_of(slab * g + quarter * j, quarter), quarter)
            down.append(
                remote(
                    src.at[:, 0:half, :], ext.at[part, 2 * half : 3 * half, :],
                    base + 1 + j, base + 1 + 2 * g + j, (v, strip_before, 1),
                )
            )
            up.append(
                remote(
                    src.at[:, half:strip, :], ext.at[part, 0:half, :],
                    base + 3 + j, base + 1 + 2 * g + j, (v, strip_after, 0),
                )
            )
        return across, down, up

    def spread_start(copies):
        across, down, up = copies

        @pl.when(s > 0)
        def _():
            for copy in down:
                copy.start()

        @pl.when(s < strips - 1)
        def _():
            for copy in up:
                copy.start()

        across.start()

    def across_arrive(ext, base):
        theirs = pl.ds(pl.multiple_of(slab * (1 - g), slab), slab)
        remote(
            ext.at[mine, pl.ds(lay, strip), :], ext.at[theirs, pl.ds(lay, strip), :],
            base, base, sibling,
        ).wait_recv()

    def spread_arrive(ext, base, c, j):
        part = pl.ds(c * slab + j * quarter, quarter)
        number = base + 1 + 2 * c + j

        @pl.when(jnp.logical_and(g == 0, s > 0))
        def _():
            remote(
                ext.at[part, half : 2 * half, :], ext.at[part, 0:half, :],
                number, number, sibling,
            ).wait_recv()

        @pl.when(jnp.logical_and(g == 1, s < strips - 1))
        def _():
            remote(
                ext.at[part, half : 2 * half, :], ext.at[part, 2 * half : 3 * half, :],
                number, number, sibling,
            ).wait_recv()

    def spread_sent(copies):
        across, down, up = copies
        across.wait_send()

        @pl.when(s > 0)
        def _():
            for copy in down:
                copy.wait_send()

        @pl.when(s < strips - 1)
        def _():
            for copy in up:
                copy.wait_send()

    est_copies = spread(first, 0, first.at[mine, pl.ds(lay, strip), :])
    spread_start(est_copies)
    view_copies = spread(vext, 5, views.at[0])
    quarter_here = pl.ds(pl.multiple_of(quarter * vb, quarter), quarter)
    mast_copy = remote(
        est.at[quarter_here, pl.ds(pl.multiple_of(half * (1 - g), half), half), :],
        mast, 10, 10, sibling,
    )

    @pl.when(g == va)
    def _():
        mast_copy.start()
        mast[...] = est[quarter_here, pl.ds(pl.multiple_of(half * g, half), half), :]

    x_forward, = band(kern, 2, [(width, width, 1, reach)])
    x_backward, = band(kern, 2, [(width, width, -1, reach)])
    high, low = split(x_forward)
    xfor[:, :width] = high
    xfor[:, width:] = low
    high, low = split(x_backward)
    xback[:width, :width] = high
    xback[:width, width:] = low
    xback[width:, :width] = high
    xback[width:, width:] = jnp.zeros((width, width), BF16)
    z_mats = band(kern, 0, [(planes, planes, -1, reach), (planes, planes, 1, reach)])
    r_mats = band(
        kern, 1, [(half, 3 * half, -1, reach - half), (half, 3 * half, 1, reach + half)]
    )
    for way in range(2):
        high, low = split(z_mats[way])
        zmat[way, :planes, :] = high
        zmat[way, planes:, :] = low
        high, low = split(r_mats[way])
        rmat[way, :half, :] = high
        rmat[way, half:, :] = low

    def piece(k, h):
        return pl.ds(pl.multiple_of(quarter * other_view(k) + group * h, group), group)

    def halo(ext, base, k, h):
        part = piece(k, h)
        src = ext.at[part, half : 2 * half, :]
        at = base + 4 * k + 2 * h
        return (
            remote(src, ext.at[part, 2 * half : 3 * half, :], at, at, before),
            remote(src, ext.at[part, 0:half, :], at + 1, at + 1, after),
        )

    def halo_start(copies):
        down, up = copies

        @pl.when(has_prev)
        def _():
            down.start()

        @pl.when(has_next)
        def _():
            up.start()

    def halo_arrive(copies):
        down, up = copies

        @pl.when(has_next)
        def _():
            down.wait_recv()

        @pl.when(has_prev)
        def _():
            up.wait_recv()

    def halo_sent(copies):
        down, up = copies

        @pl.when(has_prev)
        def _():
            down.wait_send()

        @pl.when(has_next)
        def _():
            up.wait_send()

    def along_rows(ext, way, plane):
        mat = rmat[way]
        parts = []
        for i in range(0, group, 2):
            both = dot(mat, jnp.concatenate([ext[plane + i], ext[plane + i + 1]], axis=1))
            both = both[:half] + both[half:]
            parts += [both[:, :width], both[:, width:]]
        return jnp.concatenate(parts, axis=0)

    def forward(ext, plane):
        both = dot(along_rows(ext, 0, plane).astype(BF16), xfor[...])
        mid[pl.ds(pl.multiple_of(plane * half, group * half), group * half), :] = (
            both[:, :width] + both[:, width:]
        )

    def backward(ext, plane):
        high, low = split(along_rows(ext, 1, plane))
        both = dot(jnp.concatenate([high, low], axis=1), xback[...])
        return both[:, :width] + both[:, width:]

    def loop(steps, body, wide=1):
        def step(i, carry):
            for n in range(wide):
                body(wide * i + n)
            return carry

        lax.fori_loop(0, steps // wide, step, 0)

    block = lax.div(q * half, BLOCK)
    weight = cov[v, block, 0].astype(F32)
    count = jnp.float32(0.0)
    for n in range(4):
        count = count + cov[n, block, 0].astype(F32)

    across_arrive(first, 0)
    for j in range(2):
        for c in range(2):
            spread_arrive(first, 0, c, j)
            if (j, c) == (1, 1):
                spread_start(view_copies)
            for h in range(quarter // group):
                forward(first, c * slab + j * quarter + group * h)

    lay_views.wait()
    across_arrive(vext, 5)
    blank = jnp.zeros((slab * half, width), F32)
    data[: slab * half, :] = blank
    data[(slab + planes) * half :, :] = blank
    row = lax.broadcasted_iota(jnp.int32, (half, 3 * half), 0)
    col = lax.broadcasted_iota(jnp.int32, (half, 3 * half), 1)
    pick_rows = (col == row + half + shifts[0, 1]).astype(F32).astype(BF16)
    row = lax.broadcasted_iota(jnp.int32, (width, width), 0)
    col = lax.broadcasted_iota(jnp.int32, (width, width), 1)
    pick_x = (row == col + shifts[0, 2]).astype(F32).astype(BF16)

    def window(plane):
        parts = []
        for j in range(0, group, 2):
            pair = jnp.concatenate([vext[plane + j], vext[plane + j + 1]], axis=1)
            both = dot(pick_rows, pair)
            parts += [both[:, :width], both[:, width:]]
        moved = dot(jnp.concatenate(parts, axis=0).astype(BF16), pick_x)
        data[(slab + plane) * half : (slab + plane + group) * half, :] = moved

    for j in range(2):
        for c in range(2):
            spread_arrive(vext, 5, c, j)
            for h in range(quarter // group):
                window(c * slab + j * quarter + group * h)

    shifted = (slab + shifts[0, 0]) * half

    def column(ref, y):
        return jnp.concatenate(
            [ref[pl.ds(y, planes, stride=half), :], ref[pl.ds(y + 1, planes, stride=half), :]],
            axis=1,
        )

    def along_planes(i):
        for j in range(0, 4, 2):
            y = 4 * i + j
            both = dot(zmat[0], column(mid, y).astype(BF16))
            predicted = both[:planes] + both[planes:]
            ratio = column(data, y + shifted) / (predicted + 0.05)
            both = dot(zmat[1], ratio.astype(BF16))
            both = both[:planes] + both[planes:]
            back[pl.ds(y, planes, stride=half), :] = both[:, :width]
            back[pl.ds(y + 1, planes, stride=half), :] = both[:, width:]

    pieces = group * half
    order = ((3, 0), (3, 1), (1, 0), (2, 1), (1, 1), (2, 0), (0, 0), (0, 1))
    place_rows = pl.ds(pl.multiple_of(half * g, half), half)
    halos, sends, results = [], [], []

    for step in range(ITERS):
        loop(half // 4, along_planes, 2)
        ext = bext.at[step]
        last = step == ITERS - 1
        copies = {}
        for k, h in order:
            part = piece(k, h)
            at = pl.multiple_of((quarter * other_view(k) + group * h) * half, pieces)
            ext[part, half : 2 * half, :] = (
                back[pl.ds(at, pieces), :].reshape(group, half, width).astype(BF16)
            )
            copies[k, h] = halo(ext, 11 + 16 * step, k, h)
            halo_start(copies[k, h])
        halos += list(copies.values())
        base = 59 + 6 * step
        sums = {}
        for h in range(2):
            sums[3, h] = remote(
                term.at[step, h], relay.at[step, h], base + h, base + h,
                (other_view(1 + h), s, g),
            )
            for k in (1, 2):
                at = base + 2 * k + h
                sums[k, h] = remote(
                    term.at[step, 2 * k + h], slots.at[step, k - 1, h], at, at,
                    (other_view(k), s, g),
                )
        sends += list(sums.values())
        for k, h in order:
            halo_arrive(copies[k, h])
            value = weight * backward(ext, quarter * other_view(k) + group * h)
            if k == 0:
                own[h] = value
                continue
            if (k, h) in ((1, 1), (2, 0)):
                sums[3, h].wait_recv()
                value = value + relay[step, h]
            term[step, h if k == 3 else 2 * k + h] = value
            sums[k, h].start()
        if step == 0:

            @pl.when(g != va)
            def _():
                mast_copy.wait_recv()

        here = quarter * v
        ext = None if last else fext.at[step + 1]
        news, copies = {}, {}
        for h in range(2):
            sums[1, h].wait_recv()
            sums[2, h].wait_recv()
            total = own[h] + slots[step, 0, h] + slots[step, 1, h]
            at = slice(group * h, group * (h + 1))
            field = mast[at] * total.reshape(group, half, width) / count
            if last:
                fin[at] = field
                place = out.at[
                    pl.ds(pl.multiple_of(quarter * vb + group * h, group), group), place_rows, :
                ]
                arrive = 77 + 4 * vb + 2 * g + h
                copies = [
                    remote(fin.at[at], place, 77 + 2 * k + h, arrive, (other_view(k), s, va))
                    for k in range(3)
                ]
                copies[1].start()
                copies[2].start()
                sends += copies[1:]
                results.append((copies[0], pltpu.make_async_copy(fin.at[at], place, local.at[h])))

                @pl.when(g == va)
                def _():
                    results[-1][1].start()

                @pl.when(g != va)
                def _():
                    results[-1][0].start()

                continue
            mast[at] = field
            part = piece(0, h)
            ext[part, half : 2 * half, :] = field.astype(BF16)
            src = ext.at[part, half : 2 * half, :]
            for k in (1, 2):
                at = 71 + 2 * (k - 1) + h
                sent = remote(src, src, at, at, (other_view(k), s, g))
                sent.start()
                sends.append(sent)
            copies[0, h] = halo(ext, 43, 0, h)
            halo_start(copies[0, h])
        if last:
            break

        def gathered(k, h):
            src = ext.at[piece(k, h), half : 2 * half, :]
            at = 71 + 2 * (k - 1) + h
            remote(src, src, at, at, sibling).wait_recv()
            if (k, h) in ((1, 0), (2, 1)):
                sent = remote(src, src, 75 + h, 75 + h, (other_view(3 - k), s, g))
                sent.start()
                sends.append(sent)
            copies[k, h] = halo(ext, 43, k, h)
            halo_start(copies[k, h])

        def blurred(k, h):
            halo_arrive(copies[k, h])
            forward(ext, quarter * other_view(k) + group * h)

        for k, h in ((1, 0), (2, 0), (1, 1), (2, 1)):
            gathered(k, h)
        blurred(0, 0)
        blurred(0, 1)
        gathered(3, 0)
        blurred(1, 0)
        blurred(2, 0)
        gathered(3, 1)
        for k, h in ((1, 1), (2, 1), (3, 0), (3, 1)):
            blurred(k, h)
        halos += list(copies.values())

    same = 1 - lax.rem(g + va, 2)
    from_b = lax.rem(vb + same, 2)
    from_h = 1 - same
    onward = 2 * lax.rem(va + same, 2) + lax.rem(vb + 1 - same, 2)

    def spot(b, c, h):
        first_plane = pl.multiple_of(quarter * b + group * h, group)
        return out.at[pl.ds(first_plane, group), half * c : half * (c + 1), :]

    for c in range(2):
        at = 77 + 4 * from_b + 2 * c + from_h
        target = spot(from_b, c, from_h)
        sent = remote(target, target, 83 + c, at, (onward, s, g))
        sent.wait_recv()
        sent.start()
        sends.append(sent)
    for h in range(2):
        for b in range(2):
            for c in range(2):
                itself = jnp.logical_and(v == 2 * g + b, g == c)
                done = jnp.logical_and(from_b == b, from_h == h)

                @pl.when(jnp.logical_not(jnp.logical_or(itself, done)))
                def _():
                    target = spot(b, c, h)
                    at = 77 + 4 * b + 2 * c + h
                    remote(target, target, at, at, sibling).wait_recv()

    @pl.when(g == va)
    def _():
        mast_copy.wait_send()
        for _, copy in results:
            copy.wait()

    @pl.when(g != va)
    def _():
        for copy, _ in results:
            copy.wait_send()

    spread_sent(est_copies)
    spread_sent(view_copies)
    for copies in halos:
        halo_sent(copies)
    for sent in sends:
        sent.wait_send()


def on_device(strips, estimate, views, shifts, kernels, coverage):
    slab, strip, width = estimate.shape
    half, planes = strip // 2, 2 * slab
    quarter = planes // 4
    hbm = pl.BlockSpec(memory_space=pl.ANY)
    smem = pl.BlockSpec(memory_space=pltpu.SMEM)
    rows = planes * half
    scratch = [
        pltpu.VMEM(estimate.shape, F32),
        pltpu.VMEM((ITERS, planes, 3 * half, width), BF16),
        pltpu.VMEM((ITERS, planes, 3 * half, width), BF16),
        pltpu.VMEM((planes, 3 * half, width), BF16),
        pltpu.VMEM((2 * rows, width), F32),
        pltpu.VMEM((rows, width), F32),
        pltpu.VMEM((rows, width), F32),
        pltpu.VMEM((quarter, half, width), F32),
        pltpu.VMEM((2, quarter * half // 2, width), F32),
        pltpu.VMEM((ITERS, 6, quarter * half // 2, width), F32),
        pltpu.VMEM((ITERS, 2, 2, quarter * half // 2, width), F32),
        pltpu.VMEM((ITERS, 2, quarter * half // 2, width), F32),
        pltpu.VMEM((quarter, half, width), F32),
        pltpu.VMEM((2, 2 * half, 3 * half), BF16),
        pltpu.VMEM((width, 2 * width), BF16),
        pltpu.VMEM((2 * width, 2 * width), BF16),
        pltpu.VMEM((2, 2 * planes, planes), BF16),
        pltpu.SemaphoreType.DMA((85,)),
        pltpu.SemaphoreType.DMA((85,)),
        pltpu.SemaphoreType.DMA((2,)),
    ]
    return pl.pallas_call(
        functools.partial(kernel, strips),
        out_shape=jax.ShapeDtypeStruct(estimate.shape, F32),
        in_specs=[smem, smem, smem, hbm, hbm],
        out_specs=hbm,
        scratch_shapes=scratch,
        compiler_params=pltpu.CompilerParams(
            collective_id=0, has_side_effects=True, vmem_limit_bytes=62 * 1024 * 1024
        ),
        cost_estimate=pl.CostEstimate(
            flops=12 * 2 * rows * width * 100, bytes_accessed=8 * rows * width, transcendentals=0
        ),
    )(coverage, shifts, kernels, estimate, views)


def solution(mesh):
    placed = (
        P("gz", "xy", None),
        P("view", "gz", "xy", None),
        P("view", None),
        P("view", None, None),
        P(),
    )
    return jax.shard_map(
        functools.partial(on_device, mesh.shape["xy"]),
        mesh=mesh, in_specs=placed, out_specs=P("gz", "xy", None), check_vma=False,
    )
```

time: 93.5 us -> 83.3 us (0.89)
  Pallas kernels: 88.7 us -> 78.8 us
    pallas_call x1, Pallas kernels: 88.7 us -> 78.8 us  [on_device(): pl.pallas_call(functools.partial(kernel, strips), out_shape=jax.ShapeDtyp...]
    unnamed x11 -> x5, local copies, waits for them, and re-layouts: 4.59 us -> 4.28 us
where the time goes in v4:
time: 83.3 us; the launch traced here: 83.1 us
  Pallas kernels  78.8 us (95%)
  local copies, waits for them, and re-layouts  4.28 us (5%)
    pallas_call x1, Pallas kernels, on_device(): pl.pallas_call(functools.partial(kernel, strips), out_shape=jax.ShapeDtyp...  78.8 us
    unnamed x5, local copies, waits for them, and re-layouts  4.28 us

profile of v4, /device:TPU:9, one launch (start us, length us, event | category | flops | bytes accessed | tf_op | source)
XLA Modules:
  0.0 83.1 jit_solution(4409853100649388619)
XLA Ops:
  0.0 0.0 copy-start
  0.0 1.3 %copy.7.kern = f32[1,3,63]{2,1,0:T(4,128)} copy(f32[1,3,63]{2,0,1:T(1,128)} %param.8) | data formatting | bytes 1512 | tf_op args[3]
  1.3 0.0 copy-done
  1.3 0.7 copy.6.cov
  2.0 78.8 %shard_map.55 = f32[32,64,128]{2,1,0:T(8,128)} custom-call(s32[4,2,1]{2,1,0:T(2,128)} %copy.6.cov, s32[1,3]{1,0:T(1,128)} %shifts.1, f32[1,3,63]{2,1,0:T(4,128)} %copy.7.kern, f32[32,64,128]{2,1,0:T(8,128)} %given.1, bf16[1,32,64,128]{3,2,1,0:T(8,128)(2,1)} %views.1), custom_call_target="tpu_custom_call" | custom-call | flops 629145600 | bytes 2097152 | tf_op jit(solution)/shard_map/pallas_call | solution.py:578
  80.7 2.3 %copy.9 = f32[32,64,128]{2,1,0:T(8,128)} copy(f32[32,64,128]{2,1,0:T(8,128)} %shard_map.55) | data formatting | bytes 2097152
Async XLA Ops:
  0.0 1.3 %copy-start = (s32[4,2,1]{0,2,1:T(1,128)S(1)}, s32[4,2,1]{0,2,1:T(1,128)}, u32[]{:S(2)}) copy-start(s32[4,2,1]{0,2,1:T(1,128)} %param.9) | copy-start | bytes 100

commit v5 on v4

--- a/solution.py
+++ b/solution.py
@@ -19,6 +19,35 @@
     return high, (value - high.astype(F32)).astype(BF16)
 
 
+def encode(value):
+    groups = value.reshape(-1, 8, value.shape[-1])
+    top = jnp.maximum(jnp.max(groups, axis=0), 1e-30)
+    whole = (groups * (32767.0 / top)[None] + 0.5).astype(jnp.int32)
+    return whole.reshape(value.shape).astype(jnp.int16), top
+
+
+def decode(code, top):
+    groups = code.astype(jnp.int32).astype(F32).reshape(-1, 8, code.shape[-1])
+    return (groups * (top * (1.0 / 32767.0))[None]).reshape(code.shape)
+
+
+class Pair:
+    def __init__(self, *copies):
+        self.copies = copies
+
+    def start(self):
+        for copy in self.copies:
+            copy.start()
+
+    def wait_recv(self):
+        for copy in self.copies:
+            copy.wait_recv()
+
+    def wait_send(self):
+        for copy in self.copies:
+            copy.wait_send()
+
+
 def dot(a, b):
     return jnp.dot(a, b, preferred_element_type=F32)
 
@@ -32,7 +61,7 @@
 
     def add_tap(tap, carry):
         total, mats = carry
-        value = kern[0, axis, tap]
+        value = kern[axis, 0, tap]
         return total + value, tuple(
             mat + jnp.where(mark == tap, value, 0.0) for mat, mark in zip(mats, marks)
         )
@@ -44,8 +73,9 @@
 
 def kernel(
     strips, cov, shifts, kern, given, views, out,
-    est, fext, bext, vext, data, mid, back, mast, own, term, slots, relay, fin,
-    rmat, xfor, xback, zmat, send, recv, local,
+    est, fext, bext, vext, data, mid, back, mast, own, term, term_top, inbox, inbox_top,
+    fin, fin_top, final, final_top,
+    rmat, xfor, xback, zmat, send, recv, send_top, recv_top, local,
 ):
     slab, strip, width = est.shape
     half = strip // 2
@@ -94,6 +124,15 @@
         return pltpu.make_async_remote_copy(
             src_ref=src, dst_ref=dst, send_sem=send.at[send_id], recv_sem=recv.at[recv_id],
             device_id=device, device_id_type=MESH,
+        )
+
+    def coded(src, src_top, dst, dst_top, send_id, recv_id, device):
+        return Pair(
+            remote(src, dst, send_id, recv_id, device),
+            pltpu.make_async_remote_copy(
+                src_ref=src_top, dst_ref=dst_top, send_sem=send_top.at[send_id],
+                recv_sem=recv_top.at[recv_id], device_id=device, device_id_type=MESH,
+            ),
         )
 
     mine = pl.ds(pl.multiple_of(slab * g, slab), slab)
@@ -315,10 +354,10 @@
         lax.fori_loop(0, steps // wide, step, 0)
 
     block = lax.div(q * half, BLOCK)
-    weight = cov[v, block, 0].astype(F32)
+    weight = cov[block, 0, v].astype(F32)
     count = jnp.float32(0.0)
     for n in range(4):
-        count = count + cov[n, block, 0].astype(F32)
+        count = count + cov[block, 0, n].astype(F32)
 
     across_arrive(first, 0)
     for j in range(2):
@@ -377,7 +416,6 @@
 
     pieces = group * half
     order = ((3, 0), (3, 1), (1, 0), (2, 1), (1, 1), (2, 0), (0, 0), (0, 1))
-    place_rows = pl.ds(pl.multiple_of(half * g, half), half)
     halos, sends, results = [], [], []
 
     for step in range(ITERS):
@@ -396,16 +434,13 @@
         halos += list(copies.values())
         base = 59 + 6 * step
         sums = {}
-        for h in range(2):
-            sums[3, h] = remote(
-                term.at[step, h], relay.at[step, h], base + h, base + h,
-                (other_view(1 + h), s, g),
-            )
-            for k in (1, 2):
-                at = base + 2 * k + h
-                sums[k, h] = remote(
-                    term.at[step, 2 * k + h], slots.at[step, k - 1, h], at, at,
-                    (other_view(k), s, g),
+        for k in (3, 1, 2):
+            for h in range(2):
+                n = h if k == 3 else 2 * k + h
+                sums[k, h] = coded(
+                    term.at[step, n], term_top.at[step, n],
+                    inbox.at[step, n], inbox_top.at[step, n],
+                    base + n, base + n, (other_view(1 + h if k == 3 else k), s, g),
                 )
         sends += list(sums.values())
         for k, h in order:
@@ -416,8 +451,9 @@
                 continue
             if (k, h) in ((1, 1), (2, 0)):
                 sums[3, h].wait_recv()
-                value = value + relay[step, h]
-            term[step, h if k == 3 else 2 * k + h] = value
+                value = value + decode(inbox[step, h], inbox_top[step, h])
+            n = h if k == 3 else 2 * k + h
+            term[step, n], term_top[step, n] = encode(value)
             sums[k, h].start()
         if step == 0:
 
@@ -431,31 +467,29 @@
         for h in range(2):
             sums[1, h].wait_recv()
             sums[2, h].wait_recv()
-            total = own[h] + slots[step, 0, h] + slots[step, 1, h]
+            total = own[h]
+            for n in (2 + h, 4 + h):
+                total = total + decode(inbox[step, n], inbox_top[step, n])
             at = slice(group * h, group * (h + 1))
             field = mast[at] * total.reshape(group, half, width) / count
             if last:
-                fin[at] = field
-                place = out.at[
-                    pl.ds(pl.multiple_of(quarter * vb + group * h, group), group), place_rows, :
-                ]
-                arrive = 77 + 4 * vb + 2 * g + h
+                fin[h], fin_top[h] = encode(field.reshape(pieces, width))
+                n = 4 * vb + 2 * g + h
                 copies = [
-                    remote(fin.at[at], place, 77 + 2 * k + h, arrive, (other_view(k), s, va))
+                    coded(
+                        fin.at[h], fin_top.at[h], final.at[n], final_top.at[n],
+                        77 + 2 * k + h, 77 + n, (other_view(k), s, va),
+                    )
                     for k in range(3)
                 ]
                 copies[1].start()
                 copies[2].start()
                 sends += copies[1:]
-                results.append((copies[0], pltpu.make_async_copy(fin.at[at], place, local.at[h])))
-
-                @pl.when(g == va)
-                def _():
-                    results[-1][1].start()
+                results.append(copies[0])
 
                 @pl.when(g != va)
                 def _():
-                    results[-1][0].start()
+                    results[-1].start()
 
                 continue
             mast[at] = field
@@ -504,38 +538,50 @@
     from_h = 1 - same
     onward = 2 * lax.rem(va + same, 2) + lax.rem(vb + 1 - same, 2)
 
-    def spot(b, c, h):
-        first_plane = pl.multiple_of(quarter * b + group * h, group)
-        return out.at[pl.ds(first_plane, group), half * c : half * (c + 1), :]
-
     for c in range(2):
-        at = 77 + 4 * from_b + 2 * c + from_h
-        target = spot(from_b, c, from_h)
-        sent = remote(target, target, 83 + c, at, (onward, s, g))
+        n = 4 * from_b + 2 * c + from_h
+        sent = coded(
+            final.at[n], final_top.at[n], final.at[n], final_top.at[n],
+            83 + c, 77 + n, (onward, s, g),
+        )
         sent.wait_recv()
         sent.start()
         sends.append(sent)
     for h in range(2):
         for b in range(2):
             for c in range(2):
+                n = 4 * b + 2 * c + h
                 itself = jnp.logical_and(v == 2 * g + b, g == c)
                 done = jnp.logical_and(from_b == b, from_h == h)
 
+                def place(code, top):
+                    first_plane = quarter * b + group * h
+                    out[first_plane : first_plane + group, half * c : half * (c + 1), :] = decode(
+                        code, top
+                    ).reshape(group, half, width)
+
                 @pl.when(jnp.logical_not(jnp.logical_or(itself, done)))
                 def _():
-                    target = spot(b, c, h)
-                    at = 77 + 4 * b + 2 * c + h
-                    remote(target, target, at, at, sibling).wait_recv()
+                    coded(
+                        final.at[n], final_top.at[n], final.at[n], final_top.at[n],
+                        77 + n, 77 + n, sibling,
+                    ).wait_recv()
+
+                @pl.when(itself)
+                def _():
+                    place(fin[h], fin_top[h])
+
+                @pl.when(jnp.logical_not(itself))
+                def _():
+                    place(final[n], final_top[n])
 
     @pl.when(g == va)
     def _():
         mast_copy.wait_send()
-        for _, copy in results:
-            copy.wait()
 
     @pl.when(g != va)
     def _():
-        for copy, _ in results:
+        for copy in results:
             copy.wait_send()
 
     spread_sent(est_copies)
@@ -550,7 +596,7 @@
     slab, strip, width = estimate.shape
     half, planes = strip // 2, 2 * slab
     quarter = planes // 4
-    hbm = pl.BlockSpec(memory_space=pl.ANY)
+    hbm = pl.BlockSpec(memory_space=pltpu.HBM)
     smem = pl.BlockSpec(memory_space=pltpu.SMEM)
     rows = planes * half
     scratch = [
@@ -563,14 +609,20 @@
         pltpu.VMEM((rows, width), F32),
         pltpu.VMEM((quarter, half, width), F32),
         pltpu.VMEM((2, quarter * half // 2, width), F32),
-        pltpu.VMEM((ITERS, 6, quarter * half // 2, width), F32),
-        pltpu.VMEM((ITERS, 2, 2, quarter * half // 2, width), F32),
-        pltpu.VMEM((ITERS, 2, quarter * half // 2, width), F32),
-        pltpu.VMEM((quarter, half, width), F32),
+        pltpu.VMEM((ITERS, 6, quarter * half // 2, width), jnp.int16),
+        pltpu.VMEM((ITERS, 6, 8, width), F32),
+        pltpu.VMEM((ITERS, 6, quarter * half // 2, width), jnp.int16),
+        pltpu.VMEM((ITERS, 6, 8, width), F32),
+        pltpu.VMEM((2, quarter * half // 2, width), jnp.int16),
+        pltpu.VMEM((2, 8, width), F32),
+        pltpu.VMEM((8, quarter * half // 2, width), jnp.int16),
+        pltpu.VMEM((8, 8, width), F32),
         pltpu.VMEM((2, 2 * half, 3 * half), BF16),
         pltpu.VMEM((width, 2 * width), BF16),
         pltpu.VMEM((2 * width, 2 * width), BF16),
         pltpu.VMEM((2, 2 * planes, planes), BF16),
+        pltpu.SemaphoreType.DMA((85,)),
+        pltpu.SemaphoreType.DMA((85,)),
         pltpu.SemaphoreType.DMA((85,)),
         pltpu.SemaphoreType.DMA((85,)),
         pltpu.SemaphoreType.DMA((2,)),
@@ -579,15 +631,15 @@
         functools.partial(kernel, strips),
         out_shape=jax.ShapeDtypeStruct(estimate.shape, F32),
         in_specs=[smem, smem, smem, hbm, hbm],
-        out_specs=hbm,
+        out_specs=pl.BlockSpec(memory_space=pltpu.VMEM),
         scratch_shapes=scratch,
         compiler_params=pltpu.CompilerParams(
-            collective_id=0, has_side_effects=True, vmem_limit_bytes=62 * 1024 * 1024
+            collective_id=0, has_side_effects=True, vmem_limit_bytes=40 * 1024 * 1024
         ),
         cost_estimate=pl.CostEstimate(
             flops=12 * 2 * rows * width * 100, bytes_accessed=8 * rows * width, transcendentals=0
         ),
-    )(coverage, shifts, kernels, estimate, views)
+    )(coverage.transpose(1, 2, 0), shifts, kernels.transpose(1, 0, 2), estimate, views)
 
 
 def solution(mesh):

time: 83.3 us -> 73.2 us (0.88)
  Pallas kernels: 78.8 us -> 68.8 us
    pallas_call x1, Pallas kernels: 78.8 us -> 68.8 us  [on_device(): pl.pallas_call(functools.partial(kernel, strips), out_shape=jax.ShapeDtyp...]
    unnamed x5 -> x11, local copies, waits for them, and re-layouts: 4.28 us -> 3.93 us
where the time goes in v5:
time: 73.2 us; the launch traced here: 72.7 us
  Pallas kernels  68.8 us (94%)
  local copies, waits for them, and re-layouts  3.93 us (5%)
    pallas_call x1, Pallas kernels, on_device(): pl.pallas_call(functools.partial(kernel, strips), out_shape=jax.ShapeDtyp...  68.8 us
    unnamed x11, local copies, waits for them, and re-layouts  3.93 us

profile of v5, /device:TPU:9, one launch (start us, length us, event | category | flops | bytes accessed | tf_op | source)
XLA Modules:
  0.0 72.7 jit_solution(15782142195921303381)
XLA Ops:
  0.0 0.0 copy-start.2
  0.0 0.0 copy-start.3
  0.0 0.0 copy-start.4
  0.0 0.7 copy-done.2
  0.7 0.0 copy-done.3
  0.7 0.0 copy-done.4
  0.7 0.0 copy-start
  0.7 1.2 %copy-done = f32[32,64,128]{2,1,0:T(8,128)S(1)} copy-done((f32[32,64,128]{2,1,0:T(8,128)S(1)}, f32[32,64,128]{2,1,0:T(8,128)}, u32[]{:S(2)}) %copy-start) | copy-done | bytes 1048600
  1.9 0.0 copy-start.1
  1.9 1.0 %copy-done.1 = bf16[1,32,64,128]{3,2,1,0:T(8,128)(2,1)S(1)} copy-done((bf16[1,32,64,128]{3,2,1,0:T(8,128)(2,1)S(1)}, bf16[1,32,64,128]{3,2,1,0:T(8,128)(2,1)}, u32[]{:S(2)}) %copy-start.1) | copy-done | bytes 524312
  3.0 68.8 %shard_map.55 = f32[32,64,128]{2,1,0:T(8,128)S(1)} custom-call(s32[2,1,4]{2,1,0:T(1,128)S(1)} %bitcast.3, s32[1,3]{1,0:T(1,128)S(1)} %copy-done.4, f32[3,1,63]{2,1,0:T(1,128)S(1)} %bitcast.2, f32[32,64,128]{2,1,0:T(8,128)S(1)} %copy-done, bf16[1,32,64,128]{3,2,1,0:T(8,128)(2,1)S(1)} %copy-done.1), custom_call_target="tpu_custom_call" | custom-call | flops 629145600 | bytes 2097152 | tf_op jit(solution)/shard_map/pallas_call | solution.py:630
  71.7 1.0 %copy.7 = f32[32,64,128]{2,1,0:T(8,128)} copy(f32[32,64,128]{2,1,0:T(8,128)S(1)} %shard_map.55) | data formatting | bytes 2097152
Async XLA Ops:
  0.0 0.7 copy-start.2
  0.0 0.7 copy-start.3
  0.0 0.7 copy-start.4
  0.7 1.2 %copy-start = (f32[32,64,128]{2,1,0:T(8,128)S(1)}, f32[32,64,128]{2,1,0:T(8,128)}, u32[]{:S(2)}) copy-start(f32[32,64,128]{2,1,0:T(8,128)} %given.1) | copy-start | bytes 3145732
  1.9 1.0 %copy-start.1 = (bf16[1,32,64,128]{3,2,1,0:T(8,128)(2,1)S(1)}, bf16[1,32,64,128]{3,2,1,0:T(8,128)(2,1)}, u32[]{:S(2)}) copy-start(bf16[1,32,64,128]{3,2,1,0:T(8,128)(2,1)} %views.1) | copy-start | bytes 1572868

commit v6 on v5

--- a/solution.py
+++ b/solution.py
@@ -634,7 +634,7 @@
         out_specs=pl.BlockSpec(memory_space=pltpu.VMEM),
         scratch_shapes=scratch,
         compiler_params=pltpu.CompilerParams(
-            collective_id=0, has_side_effects=True, vmem_limit_bytes=40 * 1024 * 1024
+            collective_id=0, has_side_effects=True, vmem_limit_bytes=56 * 1024 * 1024
         ),
         cost_estimate=pl.CostEstimate(
             flops=12 * 2 * rows * width * 100, bytes_accessed=8 * rows * width, transcendentals=0

time: 73.2 us -> 73.1 us (level)
  local copies, waits for them, and re-layouts: 3.93 us -> 2.31 us
  Pallas kernels: 68.8 us -> 70 us
    unnamed x11 -> x1, local copies, waits for them, and re-layouts: 3.93 us -> 2.31 us
    pallas_call x1, Pallas kernels: 68.8 us -> 70 us  [on_device(): pl.pallas_call(functools.partial(kernel, strips), out_shape=jax.ShapeDtyp...]
where the time goes in v6:
time: 73.1 us; the launch traced here: 72.3 us
  Pallas kernels  70 us (96%)
  local copies, waits for them, and re-layouts  2.31 us (3%)
    pallas_call x1, Pallas kernels, on_device(): pl.pallas_call(functools.partial(kernel, strips), out_shape=jax.ShapeDtyp...  70 us
    unnamed x1, local copies, waits for them, and re-layouts  2.31 us

profile of v6, /device:TPU:9, one launch (start us, length us, event | category | flops | bytes accessed | tf_op | source)
XLA Modules:
  0.0 72.3 jit_solution(9259330033961224016)
XLA Ops:
  0.0 70.0 %shard_map.55 = f32[32,64,128]{2,1,0:T(8,128)} custom-call(s32[2,1,4]{2,1,0:T(1,128)} %bitcast.3, s32[1,3]{1,0:T(1,128)} %shifts.1, f32[3,1,63]{2,1,0:T(1,128)} %bitcast.2, f32[32,64,128]{2,1,0:T(8,128)} %given.1, bf16[1,32,64,128]{3,2,1,0:T(8,128)(2,1)} %views.1), custom_call_target="tpu_custom_call" | custom-call | flops 629145600 | bytes 2097152 | tf_op jit(solution)/shard_map/pallas_call | solution.py:630
  70.0 2.3 %copy.7 = f32[32,64,128]{2,1,0:T(8,128)} copy(f32[32,64,128]{2,1,0:T(8,128)} %shard_map.55) | data formatting | bytes 2097152

commit v7 on v5

--- a/solution.py
+++ b/solution.py
@@ -84,6 +84,7 @@
     reach = (taps - 1) // 2
     quarter = planes // 4
     group = quarter // 2
+    pitch = half + 8
     v, s, g = lax.axis_index("view"), lax.axis_index("xy"), lax.axis_index("gz")
     va, vb = lax.div(v, 2), lax.rem(v, 2)
     q = 2 * s + g
@@ -336,9 +337,10 @@
 
     def forward(ext, plane):
         both = dot(along_rows(ext, 0, plane).astype(BF16), xfor[...])
-        mid[pl.ds(pl.multiple_of(plane * half, group * half), group * half), :] = (
-            both[:, :width] + both[:, width:]
-        )
+        both = both[:, :width] + both[:, width:]
+        for i in range(group):
+            at = pl.multiple_of((plane + i) * pitch, 8)
+            mid[pl.ds(at, half), :] = both[half * i : half * (i + 1)]
 
     def backward(ext, plane):
         high, low = split(along_rows(ext, 1, plane))
@@ -370,9 +372,9 @@
 
     lay_views.wait()
     across_arrive(vext, 5)
-    blank = jnp.zeros((slab * half, width), F32)
-    data[: slab * half, :] = blank
-    data[(slab + planes) * half :, :] = blank
+    blank = jnp.zeros((slab * pitch, width), F32)
+    data[: slab * pitch, :] = blank
+    data[(slab + planes) * pitch :, :] = blank
     row = lax.broadcasted_iota(jnp.int32, (half, 3 * half), 0)
     col = lax.broadcasted_iota(jnp.int32, (half, 3 * half), 1)
     pick_rows = (col == row + half + shifts[0, 1]).astype(F32).astype(BF16)
@@ -387,7 +389,9 @@
             both = dot(pick_rows, pair)
             parts += [both[:, :width], both[:, width:]]
         moved = dot(jnp.concatenate(parts, axis=0).astype(BF16), pick_x)
-        data[(slab + plane) * half : (slab + plane + group) * half, :] = moved
+        for i in range(group):
+            at = (slab + plane + i) * pitch
+            data[at : at + half, :] = moved[half * i : half * (i + 1)]
 
     for j in range(2):
         for c in range(2):
@@ -395,11 +399,11 @@
             for h in range(quarter // group):
                 window(c * slab + j * quarter + group * h)
 
-    shifted = (slab + shifts[0, 0]) * half
+    shifted = (slab + shifts[0, 0]) * pitch
 
     def column(ref, y):
         return jnp.concatenate(
-            [ref[pl.ds(y, planes, stride=half), :], ref[pl.ds(y + 1, planes, stride=half), :]],
+            [ref[pl.ds(y, planes, stride=pitch), :], ref[pl.ds(y + 1, planes, stride=pitch), :]],
             axis=1,
         )
 
@@ -411,8 +415,8 @@
             ratio = column(data, y + shifted) / (predicted + 0.05)
             both = dot(zmat[1], ratio.astype(BF16))
             both = both[:planes] + both[planes:]
-            back[pl.ds(y, planes, stride=half), :] = both[:, :width]
-            back[pl.ds(y + 1, planes, stride=half), :] = both[:, width:]
+            back[pl.ds(y, planes, stride=pitch), :] = both[:, :width]
+            back[pl.ds(y + 1, planes, stride=pitch), :] = both[:, width:]
 
     pieces = group * half
     order = ((3, 0), (3, 1), (1, 0), (2, 1), (1, 1), (2, 0), (0, 0), (0, 1))
@@ -424,11 +428,10 @@
         last = step == ITERS - 1
         copies = {}
         for k, h in order:
-            part = piece(k, h)
-            at = pl.multiple_of((quarter * other_view(k) + group * h) * half, pieces)
-            ext[part, half : 2 * half, :] = (
-                back[pl.ds(at, pieces), :].reshape(group, half, width).astype(BF16)
-            )
+            start = quarter * other_view(k) + group * h
+            for i in range(group):
+                at = pl.multiple_of((start + i) * pitch, 8)
+                ext[start + i, half : 2 * half, :] = back[pl.ds(at, half), :].astype(BF16)
             copies[k, h] = halo(ext, 11 + 16 * step, k, h)
             halo_start(copies[k, h])
         halos += list(copies.values())
@@ -604,9 +607,9 @@
         pltpu.VMEM((ITERS, planes, 3 * half, width), BF16),
         pltpu.VMEM((ITERS, planes, 3 * half, width), BF16),
         pltpu.VMEM((planes, 3 * half, width), BF16),
-        pltpu.VMEM((2 * rows, width), F32),
-        pltpu.VMEM((rows, width), F32),
-        pltpu.VMEM((rows, width), F32),
+        pltpu.VMEM((2 * planes * (half + 8), width), F32),
+        pltpu.VMEM((planes * (half + 8), width), F32),
+        pltpu.VMEM((planes * (half + 8), width), F32),
         pltpu.VMEM((quarter, half, width), F32),
         pltpu.VMEM((2, quarter * half // 2, width), F32),
         pltpu.VMEM((ITERS, 6, quarter * half // 2, width), jnp.int16),

time: 73.2 us -> 72.4 us (0.989)
  Pallas kernels: 68.8 us -> 68 us
    pallas_call x1, Pallas kernels: 68.8 us -> 68 us  [on_device(): pl.pallas_call(functools.partial(kernel, strips), out_shape=jax.ShapeDtyp...]
where the time goes in v7:
time: 72.4 us; the launch traced here: 71.9 us
  Pallas kernels  68 us (94%)
  local copies, waits for them, and re-layouts  3.93 us (5%)
    pallas_call x1, Pallas kernels, on_device(): pl.pallas_call(functools.partial(kernel, strips), out_shape=jax.ShapeDtyp...  68 us
    unnamed x11, local copies, waits for them, and re-layouts  3.93 us

profile of v7, /device:TPU:9, one launch (start us, length us, event | category | flops | bytes accessed | tf_op | source)
XLA Modules:
  0.0 71.9 jit_solution(17490829701190875872)
XLA Ops:
  0.0 0.0 copy-start.2
  0.0 0.0 copy-start.3
  0.0 0.0 copy-start.4
  0.0 0.7 copy-done.2
  0.7 0.0 copy-done.3
  0.7 0.0 copy-done.4
  0.7 0.0 copy-start
  0.7 1.2 %copy-done = f32[32,64,128]{2,1,0:T(8,128)S(1)} copy-done((f32[32,64,128]{2,1,0:T(8,128)S(1)}, f32[32,64,128]{2,1,0:T(8,128)}, u32[]{:S(2)}) %copy-start) | copy-done | bytes 1048600
  1.9 0.0 copy-start.1
  1.9 1.0 %copy-done.1 = bf16[1,32,64,128]{3,2,1,0:T(8,128)(2,1)S(1)} copy-done((bf16[1,32,64,128]{3,2,1,0:T(8,128)(2,1)S(1)}, bf16[1,32,64,128]{3,2,1,0:T(8,128)(2,1)}, u32[]{:S(2)}) %copy-start.1) | copy-done | bytes 524312
  3.0 68.0 %shard_map.55 = f32[32,64,128]{2,1,0:T(8,128)S(1)} custom-call(s32[2,1,4]{2,1,0:T(1,128)S(1)} %bitcast.3, s32[1,3]{1,0:T(1,128)S(1)} %copy-done.4, f32[3,1,63]{2,1,0:T(1,128)S(1)} %bitcast.2, f32[32,64,128]{2,1,0:T(8,128)S(1)} %copy-done, bf16[1,32,64,128]{3,2,1,0:T(8,128)(2,1)S(1)} %copy-done.1), custom_call_target="tpu_custom_call" | custom-call | flops 629145600 | bytes 2097152 | tf_op jit(solution)/shard_map/pallas_call | solution.py:633
  70.9 1.0 %copy.7 = f32[32,64,128]{2,1,0:T(8,128)} copy(f32[32,64,128]{2,1,0:T(8,128)S(1)} %shard_map.55) | data formatting | bytes 2097152
Async XLA Ops:
  0.0 0.7 copy-start.2
  0.0 0.7 copy-start.3
  0.0 0.7 copy-start.4
  0.7 1.2 %copy-start = (f32[32,64,128]{2,1,0:T(8,128)S(1)}, f32[32,64,128]{2,1,0:T(8,128)}, u32[]{:S(2)}) copy-start(f32[32,64,128]{2,1,0:T(8,128)} %given.1) | copy-start | bytes 3145732
  1.9 1.0 %copy-start.1 = (bf16[1,32,64,128]{3,2,1,0:T(8,128)(2,1)S(1)}, bf16[1,32,64,128]{3,2,1,0:T(8,128)(2,1)}, u32[]{:S(2)}) copy-start(bf16[1,32,64,128]{3,2,1,0:T(8,128)(2,1)} %views.1) | copy-start | bytes 1572868
